TPU v7x, 32 devices: a whole 2x2x4 slice. The times are simulated.
32 devices in a mesh: dp: 16 (over z, y, core), tensor: 2 (over x).
Axes of the slice: x: 2, y: 2, z: 4, core: 2. Of those that a mesh axis runs over, the one named last changes fastest.
Arguments:
- residual: bfloat16 [16384, 1024], P(('dp', 'tensor')), may hold values from -6 to 6
- ln_gain: float32 [1024], replicated, may hold values from 0.1 to 1.9
- ln_bias: float32 [1024], replicated, may hold values from -1.75 to 1.75
- w_qkv: bfloat16 [1024, 3072], P(None, 'tensor'), may hold values from -0.1875 to 0.1875
- b_qkv: float32 [3072], P('tensor'), may hold values from -3 to 3
- w_out: bfloat16 [1024, 1024], P('tensor'), may hold values from -0.75 to 0.75
- b_out: float32 [1024], replicated, may hold values from -3 to 3
- w_up: bfloat16 [1024, 4096], P(None, 'tensor'), may hold values from -0.1875 to 0.1875
- b_up: float32 [4096], P('tensor'), may hold values from -3 to 3
- w_down: bfloat16 [4096, 1024], P('tensor'), may hold values from -0.09375 to 0.09375
- b_down: float32 [1024], replicated, may hold values from -3 to 3
- grad_out: bfloat16 [16384, 1024], P(('dp', 'tensor')), may hold values from -6 to 6
Outputs:
- out: bfloat16 [16384, 1024], P(('dp', 'tensor'))
- grad_in: float32 [16384, 1024], P(('dp', 'tensor'))
- grad_ln_gain: float32 [1024], replicated
- grad_ln_bias: float32 [1024], replicated
- grad_w_qkv: float32 [1024, 3072], P(None, 'tensor')
- grad_b_qkv: float32 [3072], P('tensor')
- grad_w_out: float32 [1024, 1024], P('tensor')
- grad_b_out: float32 [1024], replicated
- grad_w_up: float32 [1024, 4096], P(None, 'tensor')
- grad_b_up: float32 [4096], P('tensor')
- grad_w_down: float32 [4096, 1024], P('tensor')
- grad_b_down: float32 [1024], replicated
All inputs are finite; a program needn't handle non-finite values.
Results may differ from a plain program's by a relative error of at most 0.012.
Values may be sent and summed in bfloat16 or wider, within the bound.
A program may use at most 256 MiB of HBM per device.

v0:
```python
from functools import partial
import math

import jax
import jax.numpy as jnp
from jax import lax
from jax.sharding import PartitionSpec as P

HD = 64
ROT = 16
LEN_MAX = 1024


epsilon = 1e-05


def contract_rows(left, right):
    return lax.dot_general(
        left, right, (((0,), (0,)), ((), ())), preferred_element_type=jnp.float32
    )


def contract_cols(left, right):
    return lax.dot_general(
        left, right, (((1,), (1,)), ((), ())), preferred_element_type=jnp.float32
    )


def turn_tables(seqlen):
    half_rot = ROT // 2
    exponent = jnp.arange(half_rot, dtype=jnp.float32) * (2.0 / ROT)
    inverse = 1.0 / 10000.0**exponent
    places = jnp.arange(seqlen, dtype=jnp.float32)
    angles = places[:, None] * inverse[None, :]
    return (jnp.cos(angles), jnp.sin(angles))


def turn_heads(heads, cosine, sine):
    half_rot = ROT // 2
    first = heads[:, :, :half_rot]
    second = heads[:, :, half_rot:ROT]
    rest = heads[:, :, ROT:]
    cos_rows = cosine[:, None, :]
    sin_rows = sine[:, None, :]
    return jnp.concatenate(
        [first * cos_rows - second * sin_rows, second * cos_rows + first * sin_rows, rest], axis=2
    )


def undo_turn(heads, cosine, sine):
    half_rot = ROT // 2
    first = heads[:, :, :half_rot]
    second = heads[:, :, half_rot:ROT]
    rest = heads[:, :, ROT:]
    cos_rows = cosine[:, None, :]
    sin_rows = sine[:, None, :]
    return jnp.concatenate(
        [first * cos_rows + second * sin_rows, second * cos_rows - first * sin_rows, rest], axis=2
    )


def shards(
    residual, ln_gain, ln_bias, w_qkv, b_qkv, w_out, b_out, w_up, b_up, w_down, b_down, grad_out
):
    rows_here = residual.shape[0]
    head_cols = w_out.shape[0]
    heads_here = head_cols // HD
    resid_wide = residual.astype(jnp.float32)
    average = jnp.mean(resid_wide, axis=1, keepdims=True)
    centered = resid_wide - average
    variance = jnp.mean(centered * centered, axis=1, keepdims=True)
    inv_std = lax.rsqrt(variance + epsilon)
    normed = centered * inv_std
    h_local = (normed * ln_gain + ln_bias).astype(jnp.bfloat16)
    h_full = lax.all_gather(h_local, "tensor", axis=0, tiled=True)
    group_rows = h_full.shape[0]
    seqlen = min(LEN_MAX, group_rows)
    seq_count = group_rows // seqlen
    qkv = jnp.dot(h_full, w_qkv, preferred_element_type=jnp.float32) + b_qkv
    up_lin = jnp.dot(h_full, w_up, preferred_element_type=jnp.float32) + b_up
    act_wide, gelu_back = jax.vjp(partial(jax.nn.gelu, approximate=False), up_lin)
    act = act_wide.astype(jnp.bfloat16)
    cosine, sine = turn_tables(seqlen)
    causal = jnp.arange(seqlen)[:, None] >= jnp.arange(seqlen)[None, :]
    scale = 1.0 / math.sqrt(HD)

    def attend(block):
        queries = turn_heads(block[:, :, 0, :], cosine, sine).astype(jnp.bfloat16)
        key_rows = turn_heads(block[:, :, 1, :], cosine, sine).astype(jnp.bfloat16)
        value_rows = block[:, :, 2, :].astype(jnp.bfloat16)
        scores = (
            jnp.einsum("qhd,khd->hqk", queries, key_rows, preferred_element_type=jnp.float32)
            * scale
        )
        scores = jnp.where(causal[None], scores, -1e30)
        peak = jnp.max(scores, axis=2, keepdims=True)
        raised = jnp.exp(scores - peak)
        totals = jnp.sum(raised, axis=2, keepdims=True)
        probs = raised / totals
        attended = jnp.einsum(
            "hqk,khd->qhd",
            probs.astype(jnp.bfloat16),
            value_rows,
            preferred_element_type=jnp.float32,
        ).astype(jnp.bfloat16)
        log_total = peak[:, :, 0] + jnp.log(totals[:, :, 0])
        return (queries, key_rows, value_rows, attended, log_total)

    blocks = qkv.reshape(seq_count, seqlen, heads_here, 3, HD)
    queries, key_rows, value_rows, attended, log_total = lax.map(attend, blocks)
    attn_rows = attended.reshape(group_rows, head_cols)
    act_part = lax.slice_in_dim(act, 0, lax.axis_size("tensor") * rows_here, axis=0)
    branch = lax.psum_scatter(
        jnp.dot(attn_rows, w_out, preferred_element_type=jnp.float32)
        + jnp.dot(act_part, w_down, preferred_element_type=jnp.float32),
        "tensor",
        scatter_dimension=0,
        tiled=True,
    )
    out = (resid_wide + branch + b_out + b_down).astype(jnp.bfloat16)
    grad_local = grad_out.astype(jnp.float32)
    grad_full = lax.all_gather(grad_out, "tensor", axis=0, tiled=True)
    grad_w_out = contract_rows(attn_rows, grad_full)
    grad_w_down = contract_rows(act, grad_full)
    d_attended = contract_cols(grad_full, w_out).astype(jnp.bfloat16)
    d_act = contract_cols(grad_full, w_down)
    d_up = gelu_back(d_act)[0].astype(jnp.bfloat16)
    grad_b_up = jnp.sum(d_up, axis=0, dtype=jnp.float32)

    def attend_back(items):
        query_part, key_part, value_part, log_part, d_part = items
        scores = (
            jnp.einsum("qhd,khd->hqk", query_part, key_part, preferred_element_type=jnp.float32)
            * scale
        )
        probs = jnp.where(causal[None], jnp.exp(scores - log_part[:, :, None]), 0.0)
        grad_values = jnp.einsum(
            "hqk,qhd->khd", probs.astype(jnp.bfloat16), d_part, preferred_element_type=jnp.float32
        )
        d_probs = jnp.einsum("qhd,khd->hqk", d_part, value_part, preferred_element_type=jnp.float32)
        d_scores = (probs * (d_probs - jnp.sum(d_probs * probs, axis=2, keepdims=True))).astype(
            jnp.bfloat16
        )
        d_query = (
            jnp.einsum("hqk,khd->qhd", d_scores, key_part, preferred_element_type=jnp.float32)
            * scale
        )
        d_key = (
            jnp.einsum("hqk,qhd->khd", d_scores, query_part, preferred_element_type=jnp.float32)
            * scale
        )
        return jnp.stack(
            [undo_turn(d_query, cosine, sine), undo_turn(d_key, cosine, sine), grad_values], axis=2
        )

    d_blocks = d_attended.reshape(seq_count, seqlen, heads_here, HD)
    d_qkv = lax.map(attend_back, (queries, key_rows, value_rows, log_total, d_blocks))
    d_qkv = d_qkv.reshape(group_rows, 3 * head_cols).astype(jnp.bfloat16)
    grad_b_qkv = jnp.sum(d_qkv, axis=0, dtype=jnp.float32)
    grad_w_qkv = contract_rows(h_full, d_qkv)
    grad_w_up = contract_rows(h_full, d_up)
    d_hidden = lax.psum_scatter(
        contract_cols(d_qkv, w_qkv) + contract_cols(d_up, w_up),
        "tensor",
        scatter_dimension=0,
        tiled=True,
    )
    gain_local = jnp.sum(d_hidden * normed, axis=0)
    bias_local = jnp.sum(d_hidden, axis=0)
    d_hat = d_hidden * ln_gain
    grad_in = grad_local + inv_std * (
        d_hat
        - jnp.mean(d_hat, axis=1, keepdims=True)
        - normed * jnp.mean(d_hat * normed, axis=1, keepdims=True)
    )
    out_bias = jnp.sum(grad_full, axis=0, dtype=jnp.float32)
    grad_w_qkv, grad_b_qkv, grad_w_out, grad_w_up, grad_b_up, grad_w_down, grad_b_out = lax.psum(
        (grad_w_qkv, grad_b_qkv, grad_w_out, grad_w_up, grad_b_up, grad_w_down, out_bias), "dp"
    )
    grad_ln_gain, grad_ln_bias = lax.psum((gain_local, bias_local), ("dp", "tensor"))
    return (
        out,
        grad_in,
        grad_ln_gain,
        grad_ln_bias,
        grad_w_qkv,
        grad_b_qkv,
        grad_w_out,
        grad_b_out,
        grad_w_up,
        grad_b_up,
        grad_w_down,
        grad_b_out,
    )


def solution(mesh):
    return jax.shard_map(
        shards,
        mesh=mesh,
        in_specs=(
            P(("dp", "tensor"), None),
            P(),
            P(),
            P(None, "tensor"),
            P("tensor"),
            P("tensor", None),
            P(),
            P(None, "tensor"),
            P("tensor"),
            P("tensor", None),
            P(),
            P(("dp", "tensor"), None),
        ),
        out_specs=(
            P(("dp", "tensor"), None),
            P(("dp", "tensor"), None),
            P(),
            P(),
            P(None, "tensor"),
            P("tensor"),
            P("tensor", None),
            P(),
            P(None, "tensor"),
            P("tensor"),
            P("tensor", None),
            P(),
        ),
        check_vma=False,
    )
```

profile of v0, /device:TPU:0, one launch (start us, length us, event | category | flops | bytes accessed | tf_op | source)
XLA Modules:
  0.0 831.6 jit_solution(7763239827454875048)
XLA Ops:
  7.2 0.0 all-gather.3.cloned.1.call-start
  7.3 1.6 convert_reduce_fusion.3
  8.9 1.6 fusion.25
  10.5 0.6 copy-done.28
  11.1 2.7 fusion.19
  13.8 0.0 all-gather.5.cloned.1.call-start
  13.8 0.7 all-gather.5.cloned.1.call-update
  14.6 1.3 iota_compare_fusion
  15.9 0.2 fusion.39
  16.1 33.6 %all-gather.3.cloned.1.call-done = bf16[1024,1024]{1,0:T(8,128)(2,1)} async-done(((bf16[512,1024]{1,0:T(8,128)(2,1)}), bf16[1024,1024]{1,0:T(8,128)(2,1)}) %all-gather.3.cloned.1.call-update) | async-done | bytes 2097168 | tf_op jit(solution)/shard_map/all_gather | solution.py:75
  49.7 6.9 convolution_add_fusion
  56.6 6.9 copy.40
  63.5 2.5 fusion.48
  66.1 0.6 copy_bitcast_fusion
  66.6 0.1 slice.111
  66.8 0.1 slice.112
  66.9 0.1 subtract_convert_fusion.1
  67.1 0.2 copy-done.2
  67.3 13.7 %select_reduce_fusion = (f32[8,1024]{1,0:T(8,128)S(1)}, f32[8,1024,1024]{1,2,0:T(8,128)}) fusion(pred[1024,1024]{0,1:T(8,128)(4,1)S(1)} %copy-done.2, bf16[1024,8,48]{0,2,1:T(8,128)(2,1)S(1)} %slice.111, bf16[1024,8,8]{0,2,1:T(8,128)(2,1)S(1)} %get-tuple-element.104, bf16[1024,8,8]{0,2,1:T(8,128)(2,1)S(1)} %get-tuple-element.105, ...), kind=kOutput, calls=%fused_computation.5 | convolution fusion | flops 1105190912 | bytes 36732928 | tf_op jit(solution)/shard_map/while/body/eval_jaxpr/qhd,khd->hqk/dot_general | solution.py:92
  81.1 14.2 %fusion = f32[8,1024]{1,0:T(8,128)S(1)} fusion(f32[8,1024,1024]{1,2,0:T(8,128)} %get-tuple-element.109, f32[8,1024]{1,0:T(8,128)S(1)} %get-tuple-element.108, pred[1024,1024]{0,1:T(8,128)(4,1)S(1)} %copy-done.2), kind=kLoop, calls=%fused_computation.6 | loop fusion | flops 33546240 | bytes 34668544 | tf_op jit(solution)/shard_map/while/body/eval_jaxpr/reduce_sum | solution.py:98
  95.3 0.6 copy-done.22
  96.0 3.2 convolution_convert_fusion
  99.2 24.2 %multiply_reduce_fusion = (f32[8,1024]{1,0:T(8,128)S(1)}, f32[8,1024,1024]{1,2,0:T(8,128)}) fusion(f32[8,1024,1024]{1,2,0:T(8,128)} %get-tuple-element.109, f32[8,1024]{1,0:T(8,128)S(1)} %log_add_fusion, pred[1024,1024]{0,1:T(8,128)(4,1)S(1)} %copy-done.3, bf16[1024,8,64]{0,2,1:T(8,128)(2,1)S(1)} %bitcast.67, f32[1024,8,3,64]{0,3,2,1:T(8,128)} %bitcast.57), kind=kOutput, calls=%fused_computation.1 | convolution fusion | flops 1115676672 | bytes 70320128 | tf_op jit(solution)/shard_map/while/body/eval_jaxpr/qhd,khd->hqk/dot_general | solution.py:140
  123.4 28.9 %multiply_convert_fusion = bf16[8,1024,1024]{1,2,0:T(8,128)(2,1)} fusion(f32[8,1024,1024]{1,2,0:T(8,128)} %get-tuple-element.111, f32[8,1024,1024]{1,2,0:T(8,128)} %get-tuple-element.109, f32[8,1024]{1,0:T(8,128)S(1)} %get-tuple-element.110, f32[8,1024]{1,0:T(8,128)S(1)} %log_add_fusion, pred[1024,1024]{0,1:T(8,128)(4,1)} %iota_compare_fusion), kind=kLoop, calls=%fused_computation | loop fusion | flops 50331648 | bytes 85000192 | tf_op jit(solution)/shard_map/while/body/eval_jaxpr/convert_element_type | solution.py:141
  152.3 10.5 %multiply_bitcast_fusion.1 = f32[1024,8,64]{0,2,1:T(8,128)} fusion(bf16[8,1024,1024]{1,2,0:T(8,128)(2,1)} %multiply_convert_fusion, bf16[1024,8,48]{0,2,1:T(8,128)(2,1)} %copy-done.10, bf16[1024,8,8]{0,2,1:T(8,128)(2,1)} %copy-done.18, bf16[1024,8,8]{0,2,1:T(8,128)(2,1)} %copy-done.19), kind=kOutput, calls=%fused_computation.61 | convolution fusion | flops 1077411840 | bytes 19922944 | tf_op jit(solution)/shard_map/while/body/eval_jaxpr/hqk,khd->qhd/dot_general | solution.py:145
  162.8 12.5 %multiply_bitcast_fusion = f32[1024,8,64]{0,2,1:T(8,128)} fusion(bf16[8,1024,1024]{1,2,0:T(8,128)(2,1)} %multiply_convert_fusion, bf16[1024,8,48]{0,2,1:T(8,128)(2,1)} %copy-done.9, bf16[1024,8,8]{0,2,1:T(8,128)(2,1)S(1)} %get-tuple-element.97, bf16[1024,8,8]{0,2,1:T(8,128)(2,1)S(1)} %get-tuple-element.96), kind=kOutput, calls=%fused_computation.60 | convolution fusion | flops 1077411840 | bytes 19922944 | tf_op jit(solution)/shard_map/while/body/eval_jaxpr/hqk,qhd->khd/dot_general | solution.py:149
  175.3 2.4 slice.89
  177.8 2.0 multiply_add_fusion.1
  179.8 2.4 slice.92
  182.2 15.4 %fusion.29 = bf16[1024,8,1,64]{0,3,1,2:T(8,128)(2,1)} fusion(bf16[1024,8,64]{0,2,1:T(8,128)(2,1)} %bitcast.68, f32[8,1024,1024]{1,2,0:T(8,128)} %get-tuple-element.109, f32[8,1024]{1,0:T(8,128)S(1)} %log_add_fusion, pred[1024,1024]{0,1:T(8,128)(4,1)} %iota_compare_fusion), kind=kOutput, calls=%fused_computation.64 | convolution fusion | flops 1107296256 | bytes 36732928 | tf_op jit(solution)/shard_map/while/body/eval_jaxpr/hqk,qhd->khd/dot_general | solution.py:137
  197.6 1.2 maximum_bitcast_fusion
  198.8 1.2 maximum_bitcast_fusion.1
  200.1 2.7 convert_reduce_fusion.1
  202.8 0.5 copy.48
  203.2 1.6 copy-done.11
  204.9 3.5 fusion.51
  208.4 4.5 fusion.49
  212.9 24.8 %convert_reduce_fusion = (f32[2048]{0:T(1024)S(1)}, bf16[1024,2048]{1,0:T(8,128)(2,1)S(1)}, f32[1024,2048]{1,0:T(8,128)}) fusion(f32[1024,2048]{1,0:T(8,128)S(1)} %fusion.49, f32[2048]{0:T(1024)S(1)} %copy-done.30, bf16[1024,1024]{1,0:T(8,128)(2,1)S(1)} %copy-done.13, bf16[2048,1024]{1,0:T(8,128)(2,1)S(1)} %copy-done.35), kind=kOutput, calls=%fused_computation.13 | convolution fusion | flops 4452251648 | bytes 27279360 | tf_op jit(solution)/shard_map/dot_general | solution.py:24
  237.7 2.0 copy-done.39
  239.8 6.3 convolution_add_fusion.2
  246.1 0.0 reduce-scatter.3.cloned.1.call-start
  246.1 9.9 %multiply_convert_fusion.1 = bf16[1024,2048]{1,0:T(8,128)(2,1)} fusion(f32[1024,2048]{1,0:T(8,128)} %get-tuple-element.87, f32[1024,2048]{1,0:T(8,128)} %copy-done.6, f32[2048]{0:T(1024)S(1)} %copy-done.30), kind=kLoop, calls=%fused_computation.15 | loop fusion | flops 8388608 | bytes 20979712 | tf_op jit(solution)/shard_map/convert_element_type | solution.py:82
  256.0 10.0 %fusion.50 = f32[1024,1024]{1,0:T(8,128)} fusion(bf16[1024,2048]{1,0:T(8,128)(2,1)} %multiply_convert_fusion.1, bf16[2048,1024]{1,0:T(8,128)(2,1)} %param.21), kind=kOutput, calls=%fused_computation.100 | convolution fusion | flops 4294967296 | bytes 12582912 | tf_op jit(solution)/shard_map/dot_general | solution.py:115
  266.1 16.4 %fusion.32 = bf16[8,64,1024]{2,1,0:T(8,128)(2,1)S(1)} fusion(f32[8,1024,1024]{1,2,0:T(8,128)} %get-tuple-element.109, f32[8,1024]{1,0:T(8,128)S(1)} %copy-done.23, f32[8,1024]{1,0:T(8,128)S(1)} %copy-done.21, pred[1024,1024]{0,1:T(8,128)(4,1)S(1)} %copy-done.4, f32[1024,8,3,64]{0,3,2,1:T(8,128)} %bitcast.58), kind=kOutput, calls=%fused_computation.68 | convolution fusion | flops 1116209152 | bytes 36765696 | tf_op jit(solution)/shard_map/while/body/eval_jaxpr/hqk,khd->qhd/dot_general | solution.py:100
  282.5 5.6 convolution_add_fusion.1
  288.1 0.0 all-reduce.5.cloned.1.call-start
  288.2 4.4 fusion.53
  292.5 7.3 fusion.52
  299.9 6.8 fusion.55
  306.7 6.8 fusion.54
  313.6 0.6 copy-done.26
  314.2 0.1 reduce_sum.112
  314.3 2.0 convert_reduce_fusion.2
  316.3 61.4 %all-reduce.1 = (f32[1536]{0:T(1024)}, f32[1024]{0:T(1024)S(1)}, f32[2048]{0:T(1024)}) all-reduce(f32[1536]{0:T(1024)S(1)} %reduce_sum.112, f32[1024]{0:T(1024)S(1)} %convert_reduce_fusion.2, f32[2048]{0:T(1024)S(1)} %get-tuple-element.85), channel_id=1, replica_groups=mesh['dp'=16,'tensor'=2] {'dp'}, use_global_device_ids=true, to_apply=%region_15.16 | all-reduce | flops 4608 | bytes 36864 | tf_op jit(solution)/shard_map/psum | solution.py:177
  377.7 2.6 fusion.24
  380.3 38.7 %all-reduce = (f32[1024]{0:T(1024)}, f32[1024]{0:T(1024)}) all-reduce(f32[1024]{0:T(1024)S(1)} %get-tuple-element.62, f32[1024]{0:T(1024)S(1)} %get-tuple-element.65), channel_id=1, replica_groups=mesh['dp'=16,'tensor'=2] {'dp','tensor'}, use_global_device_ids=true, to_apply=%region_10.11 | all-reduce | flops 2048 | bytes 16384 | tf_op jit(solution)/shard_map/psum | solution.py:180
  419.1 5.1 fusion.23
  424.1 382.7 %all-reduce.5.cloned.1.call-done = (f32[1024,1536]{1,0:T(8,128)}, f32[512,1024]{1,0:T(8,128)}, f32[1024,2048]{1,0:T(8,128)}, f32[2048,1024]{1,0:T(8,128)}) async-done(((f32[1024,1536]{1,0:T(8,128)}, f32[512,1024]{1,0:T(8,128)}, f32[1024,2048]{1,0:T(8,128)}, f32[2048,1024]{1,0:T(8,128)}), (f32[1024,1536]{1,0:T(8,128)}, f32[512,1024]{1,0:T(8,128)}, f32[1024,2048]{1,0:T(8,128)}, ...) | async-done | bytes 25165840 | tf_op jit(solution)/shard_map/psum | solution.py:177
  806.9 0.6 copy.71
  807.5 6.5 copy.72
  814.0 1.3 copy.73
  815.3 4.3 copy.74
  819.6 1.7 slice-done.1
  821.3 3.4 copy.75
  (100 shorter events, 0.4 us)
Async XLA Ops:
  7.2 42.6 %copy-start = (bf16[1024,1536]{1,0:T(8,128)(2,1)S(1)}, bf16[1024,1536]{1,0:T(8,128)(2,1)}, u32[]{:S(2)}) copy-start(bf16[1024,1536]{1,0:T(8,128)(2,1)} %param.15) | copy-start | bytes 9437188
  7.2 42.6 %copy-start.38 = (f32[1536]{0:T(1024)S(1)}, f32[1536]{0:T(1024)}, u32[]{:S(2)}) copy-start(f32[1536]{0:T(1024)} %param.16) | copy-start | bytes 18436
  7.2 42.5 %all-gather.3.cloned.1.call-start = ((), (), s32[]{:S(2)}) async-start(), calls=%async_computation.2 | async-start | bytes 3145728 | tf_op jit(solution)/shard_map/all_gather | solution.py:75
  8.8 1.7 copy-start.24
  10.5 0.6 copy-start.28
  13.8 82.2 %all-gather.5.cloned.1.call-start = ((), (), s32[]{:S(2)}) async-start(), calls=%async_computation.4 | async-start | bytes 3145728 | tf_op jit(solution)/shard_map/all_gather | solution.py:122
  14.5 363.1 %reduce-scatter.5.cloned.1.call-start = ((), (), s32[]{:S(2)}) async-start(), calls=%async_computation.5 | async-start | bytes 6291456 | tf_op jit(solution)/shard_map/reduce_scatter | solution.py:162
  66.0 1.2 copy-start.2
  66.8 14.3 %copy-start.10 = (bf16[1024,8,48]{0,2,1:T(8,128)(2,1)}, bf16[1024,8,48]{0,2,1:T(8,128)(2,1)S(1)}, u32[]{:S(2)}) copy-start(bf16[1024,8,48]{0,2,1:T(8,128)(2,1)S(1)} %slice.111) | copy-start | bytes 2359300
  66.9 14.1 %copy-start.9 = (bf16[1024,8,48]{0,2,1:T(8,128)(2,1)}, bf16[1024,8,48]{0,2,1:T(8,128)(2,1)S(1)}, u32[]{:S(2)}) copy-start(bf16[1024,8,48]{0,2,1:T(8,128)(2,1)S(1)} %slice.112) | copy-start | bytes 2359300
  67.1 14.0 %copy-start.18 = (bf16[1024,8,8]{0,2,1:T(8,128)(2,1)}, bf16[1024,8,8]{0,2,1:T(8,128)(2,1)S(1)}, u32[]{:S(2)}) copy-start(bf16[1024,8,8]{0,2,1:T(8,128)(2,1)S(1)} %get-tuple-element.104) | copy-start | bytes 393220
  67.1 14.0 %copy-start.19 = (bf16[1024,8,8]{0,2,1:T(8,128)(2,1)}, bf16[1024,8,8]{0,2,1:T(8,128)(2,1)S(1)}, u32[]{:S(2)}) copy-start(bf16[1024,8,8]{0,2,1:T(8,128)(2,1)S(1)} %get-tuple-element.105) | copy-start | bytes 393220
  81.0 14.2 %copy-start.20 = (f32[8,1024]{1,0:T(8,128)}, f32[8,1024]{1,0:T(8,128)S(1)}, u32[]{:S(2)}) copy-start(f32[8,1024]{1,0:T(8,128)S(1)} %get-tuple-element.108) | copy-start | bytes 98308
  95.3 0.6 copy-start.22
  95.9 3.3 copy-start.3
  99.2 24.2 %copy-start.16 = (bf16[1024,512]{0,1:T(8,128)(2,1)}, bf16[1024,512]{0,1:T(8,128)(2,1)S(1)}, u32[]{:S(2)}) copy-start(bf16[1024,512]{0,1:T(8,128)(2,1)S(1)} %convolution_convert_fusion) | copy-start | bytes 3145732
  203.2 1.6 copy-start.11
  204.9 3.5 copy-start.34
  204.9 3.5 copy-start.36
  208.4 4.6 copy-start.13
  208.4 4.6 copy-start.30
  208.4 4.5 copy-start.35
  212.9 24.8 %copy-start.6 = (f32[1024,2048]{1,0:T(8,128)}, f32[1024,2048]{1,0:T(8,128)S(1)}, u32[]{:S(2)}) copy-start(f32[1024,2048]{1,0:T(8,128)S(1)} %fusion.49) | copy-start | bytes 25165828
  237.7 2.0 copy-start.39
  246.1 173.0 %reduce-scatter.3.cloned.1.call-start = ((), (), s32[]{:S(2)}) async-start(), calls=%async_computation.3 | async-start | bytes 6291456 | tf_op jit(solution)/shard_map/reduce_scatter | solution.py:113
  256.0 10.0 %copy-start.4 = (pred[1024,1024]{0,1:T(8,128)(4,1)S(1)}, pred[1024,1024]{0,1:T(8,128)(4,1)}, u32[]{:S(2)}) copy-start(pred[1024,1024]{0,1:T(8,128)(4,1)} %iota_compare_fusion) | copy-start | bytes 3145732
  256.0 10.0 %copy-start.21 = (f32[8,1024]{1,0:T(8,128)S(1)}, f32[8,1024]{1,0:T(8,128)}, u32[]{:S(2)}) copy-start(f32[8,1024]{1,0:T(8,128)} %copy-done.20) | copy-start | bytes 98308
  256.0 10.0 %copy-start.23 = (f32[8,1024]{1,0:T(8,128)S(1)}, f32[8,1024]{1,0:T(8,128)}, u32[]{:S(2)}) copy-start(f32[8,1024]{1,0:T(8,128)} %copy-done.22) | copy-start | bytes 98308
  266.1 16.4 %copy-start.17 = (bf16[512,1024]{1,0:T(8,128)(2,1)S(1)}, bf16[512,1024]{1,0:T(8,128)(2,1)}, u32[]{:S(2)}) copy-start(bf16[512,1024]{1,0:T(8,128)(2,1)} %param.17) | copy-start | bytes 3145732
  288.1 518.7 %all-reduce.5.cloned.1.call-start = ((), (), s32[]{:S(2)}) async-start(), calls=%async_computation.6 | async-start | bytes 50331648 | tf_op jit(solution)/shard_map/psum | solution.py:177
  288.2 4.4 copy-start.12
  292.5 7.3 copy-start.7
  292.5 7.3 copy-start.14
  299.9 6.8 copy-start.37
  299.9 6.8 copy-start.40
  313.5 0.7 copy-start.26
  313.5 64.1 %copy-start.5 = (bf16[512,1024]{1,0:T(8,128)(2,1)S(1)}, bf16[512,1024]{1,0:T(8,128)(2,1)}, u32[]{:S(2)}) copy-start(bf16[512,1024]{1,0:T(8,128)(2,1)} %param.12) | copy-start | bytes 3145732
  313.5 64.1 %copy-start.25 = (f32[512]{0:T(512)S(1)}, f32[512]{0:T(512)}, u32[]{:S(2)}) copy-start(f32[512]{0:T(512)} %copy-done.24) | copy-start | bytes 6148
  313.5 64.1 %copy-start.27 = (f32[1024]{0:T(1024)S(1)}, f32[1024]{0:T(1024)}, u32[]{:S(2)}) copy-start(f32[1024]{0:T(1024)} %param.13) | copy-start | bytes 12292
  313.5 64.1 %copy-start.29 = (f32[512]{0:T(512)S(1)}, f32[512]{0:T(512)}, u32[]{:S(2)}) copy-start(f32[512]{0:T(512)} %copy-done.28) | copy-start | bytes 6148
  313.5 105.5 %copy-start.8 = (bf16[512,1024]{1,0:T(8,128)(2,1)S(1)}, bf16[512,1024]{1,0:T(8,128)(2,1)}, u32[]{:S(2)}) copy-start(bf16[512,1024]{1,0:T(8,128)(2,1)} %param.23) | copy-start | bytes 3145732
  313.6 105.5 %copy-start.31 = (f32[1024]{0:T(1024)S(1)}, f32[1024]{0:T(1024)}, u32[]{:S(2)}) copy-start(f32[1024]{0:T(1024)} %param.22) | copy-start | bytes 12292
  313.6 105.5 %copy-start.32 = (f32[1024]{0:T(1024)S(1)}, f32[1024]{0:T(1024)}, u32[]{:S(2)}) copy-start(f32[1024]{0:T(1024)} %param.18) | copy-start | bytes 12292
  377.6 429.2 %copy-start.33 = (f32[1024]{0:T(1024)}, f32[1024]{0:T(1024)S(1)}, u32[]{:S(2)}) copy-start(f32[1024]{0:T(1024)S(1)} %get-tuple-element.145) | copy-start | bytes 12292
  806.9 8.4 %slice-start.2 = ((s8[8388608]{0:T(1024)(128)(4,1)}), s8[4194304]{0:T(1024)(128)(4,1)S(1)}, s32[]{:S(2)}) async-start(s8[8388608]{0:T(1024)(128)(4,1)} %bitcast.61), calls=%async_computation.9 | async-start | bytes 8388608
  807.5 6.5 copy-start.15
  807.5 7.8 slice-start.3
  814.0 5.6 slice-start
  815.3 6.0 slice-start.1
  815.3 9.4 %copy-start.1 = (bf16[1024,1536]{1,0:T(8,128)(2,1)S(1)}, bf16[1024,1536]{1,0:T(8,128)(2,1)}, u32[]{:S(2)}) copy-start(bf16[1024,1536]{1,0:T(8,128)(2,1)} %param.15) | copy-start | bytes 9437188
Sparse Core Ops, SparseCore 0:
  13.9 35.8 all-gather.2
  51.3 33.1 all-gather.4
  246.2 54.3 reduce-scatter.4
  302.8 54.3 reduce-scatter.2
  363.0 443.7 all-reduce.4
where the time goes:
time: 842 us; the launch traced here: 832 us
  waiting for transfers between devices  417 us (50%)
  matrix products  183 us (22%)
  blocking collectives  100 us (12%)
  other arithmetic  77.5 us (9%)
  local copies, waits for them, and re-layouts  39.2 us (5%)
  between operations  14.7 us (2%)
    psum x1, waiting for transfers between devices, shards(): lax.psum((grad_w_qkv, grad_b_qkv, grad_w_out, grad_w_up, grad_b_up, grad_...  383 us
    psum x1, blocking collectives, shards(): lax.psum((grad_w_qkv, grad_b_qkv, grad_w_out, grad_w_up, grad_b_up, grad_...  61.4 us
    psum x1, blocking collectives, shards(): lax.psum((gain_local, bias_local), ('dp', 'tensor'))  38.7 us
    dot_general x4, matrix products, contract_cols(): lax.dot_general(left, right, (((1,), (1,)), ((), ())), preferred_element_...  37.8 us
    all_gather x1, waiting for transfers between devices, shards(): h_full = lax.all_gather(h_local, 'tensor', axis=0, tiled=True)  33.6 us
    convert_element_type x1, other arithmetic, attend_back(): (probs * (d_probs - jnp.sum(d_probs * probs, axis=2, keepdims=True))).ast...  28.9 us
    dot_general x4, matrix products, contract_rows(): lax.dot_general(left, right, (((0,), (0,)), ((), ())), preferred_element_...  25.3 us
    dot_general x1, matrix products, attend_back(): jnp.einsum('qhd,khd->hqk', d_part, value_part, preferred_element_type=jnp...  24.2 us
  transfers between devices with their start and end apart: 5, of which 2 were waited for; matrix products, arithmetic and copies ran while one was open for 15% of the time, Pallas kernels for 0%

commit v1 on v0

--- a/solution.py
+++ b/solution.py
@@ -1,17 +1,598 @@
-from functools import partial
+import functools
 import math
 
 import jax
 import jax.numpy as jnp
 from jax import lax
+from jax.experimental import pallas as pl
+from jax.experimental.pallas import tpu as pltpu
 from jax.sharding import PartitionSpec as P
 
 HD = 64
 ROT = 16
 LEN_MAX = 1024
-
-
 epsilon = 1e-05
+MESH = pl.DeviceIdType.MESH
+f32 = jnp.float32
+bf16 = jnp.bfloat16
+
+
+def dot(left, right):
+    return lax.dot_general(left, right, (((1,), (0,)), ((), ())), preferred_element_type=f32)
+
+
+def dot_nt(left, right):
+    return lax.dot_general(left, right, (((1,), (1,)), ((), ())), preferred_element_type=f32)
+
+
+def dot_tn(left, right):
+    return lax.dot_general(left, right, (((0,), (0,)), ((), ())), preferred_element_type=f32)
+
+
+def turn_tables(seqlen):
+    half_rot = ROT // 2
+    exponent = jnp.arange(half_rot, dtype=f32) * (2.0 / ROT)
+    inverse = 1.0 / 10000.0**exponent
+    places = jnp.arange(seqlen, dtype=f32)
+    angles = places[:, None] * inverse[None, :]
+    return (jnp.cos(angles), jnp.sin(angles))
+
+
+def turn(t, cos, sin, sign):
+    a, b = t[0:8], t[8:16]
+    return jnp.concatenate([a * cos - sign * (b * sin), b * cos + sign * (a * sin), t[16:]], axis=0)
+
+
+def attend_head(q_t, k_t, v_t, do_t, cos, sin, blk=256):
+    seq = q_t.shape[1]
+    qs = turn(q_t, cos, sin, 1.0).astype(bf16) * jnp.asarray(0.125, bf16)
+    kb = turn(k_t, cos, sin, 1.0).astype(bf16)
+    vb = v_t.astype(bf16)
+    keys, values, queries, grads = kb.T, vb.T, qs.T, do_t.T
+    nb = seq // blk
+    outs, dqs = [], []
+    dv_sum, dk_sum = [None] * nb, [None] * nb
+    for i in range(nb):
+        kk, sl = (i + 1) * blk, slice(i * blk, (i + 1) * blk)
+        s = dot(keys[:kk], qs[:, sl])
+        rows = lax.broadcasted_iota(jnp.int32, (blk, blk), 0)
+        cols = lax.broadcasted_iota(jnp.int32, (blk, blk), 1)
+        diag = jnp.where(rows <= cols, s[i * blk :], -1e30)
+        s = jnp.concatenate([s[: i * blk], diag], axis=0) if i else diag
+        p = jnp.exp(s - jnp.max(s, axis=0, keepdims=True))
+        p = p * (1.0 / jnp.sum(p, axis=0, keepdims=True))
+        pb = p.astype(bf16)
+        o = dot(vb[:, :kk], pb)
+        dp = dot(values[:kk], do_t[:, sl])
+        mean = jnp.sum(o * do_t[:, sl].astype(f32), axis=0, keepdims=True)
+        ds = (p * (dp - mean)).astype(bf16)
+        outs.append(o.astype(bf16))
+        dqs.append(dot(kb[:, :kk], ds) * 0.125)
+        dv, dk = dot(pb, grads[sl]), dot(ds, queries[sl])
+        for j in range(i + 1):
+            a, b = dv[j * blk : (j + 1) * blk], dk[j * blk : (j + 1) * blk]
+            dv_sum[j] = a if dv_sum[j] is None else dv_sum[j] + a
+            dk_sum[j] = b if dk_sum[j] is None else dk_sum[j] + b
+    dq_t = turn(jnp.concatenate(dqs, axis=1), cos, sin, -1.0)
+    dk_t = turn(jnp.concatenate(dk_sum, axis=0).T, cos, sin, -1.0)
+    dv_t = jnp.concatenate(dv_sum, axis=0).T
+    return jnp.concatenate(outs, axis=1), dq_t, dk_t, dv_t
+
+
+RW = 256
+RQ = RW // 4
+NS = 6
+KINDS = ("P", "A1", "A2", "A3", "A4", "A5", "B1", "B2", "B3", "B4", "B5a", "B5b", "G")
+KI = {k: i for i, k in enumerate(KINDS)}
+
+
+def mega_kernel(
+    n_ff, heads,
+    ffg, h, g, w_t, bq, wo, cs, ffb, ffd, resid, vecs, small_in,
+    red, out, grad_in, small_out,
+    x_buf, own, ag, fin, ra1, ra2, ra3, rb1, rb2, rb3,
+    qkv_s, do_s, dqkv_t, att_t, dh_own, br_send, br_recv, dh_send, dh_recv, ff_buf, rs_buf, sm_send, sm_recv, sums,
+    ss, rs, own_sem, loc_sem, x_ss, x_rs, ff_sem, sm_ss, sm_rs, fin_sem,
+):
+    n_at = heads // 2
+    waves = n_ff + n_at
+    dp, x = lax.axis_index("dp"), lax.axis_index("tensor")
+    c, y, z = lax.rem(dp, 2), lax.rem(dp // 2, 2), dp // 4
+    dev = lambda zz, yy, cc, xx: (zz * 4 + yy * 2 + cc, xx)
+    sib = dev(z, y, 1 - c, x)
+    yp = dev(z, 1 - y, c, x)
+    zp = dev(z + 1 - 2 * lax.rem(z, 2), y, c, x)
+    zm = dev(3 - z, y, c, x)
+    xp = dev(z, y, c, 1 - x)
+    inner = jnp.logical_or(z == 1, z == 2)
+    outer = jnp.logical_not(inner)
+
+    barrier = pltpu.get_barrier_semaphore()
+    for d in (sib, yp, zp, zm, xp):
+        pl.semaphore_signal(barrier, inc=1, device_id=d, device_id_type=MESH)
+    pl.semaphore_wait(barrier, 5)
+
+    a_mine = pl.ds(pl.multiple_of(y * RQ, RQ), RQ)
+    a_other = pl.ds(pl.multiple_of((1 - y) * RQ, RQ), RQ)
+    zi = jnp.where(z == 2, 1, 0)
+    b_mine = pl.ds(pl.multiple_of(2 * RQ + zi * RQ, RQ), RQ)
+    b_other = pl.ds(pl.multiple_of(2 * RQ + (1 - zi) * RQ, RQ), RQ)
+    b_all = pl.ds(2 * RQ, 2 * RQ)
+
+    def rc(kind, w, src, dst, device):
+        k = KI[kind]
+        return pltpu.make_async_remote_copy(
+            src_ref=src, dst_ref=dst, send_sem=ss.at[k, w], recv_sem=rs.at[k, w], device_id=device, device_id_type=MESH
+        )
+
+    def cp(kind, w):
+        s = lax.rem(w, NS)
+        if kind == "A1":
+            return rc(kind, w, x_buf.at[w, a_other], ra1.at[s], yp)
+        if kind == "A2":
+            return rc(kind, w, x_buf.at[w, a_mine], ra2.at[s], zp)
+        if kind == "A3":
+            return rc(kind, w, x_buf.at[w, a_mine], ra3.at[s], zm)
+        if kind == "A4":
+            return rc(kind, w, fin.at[w, a_mine], fin.at[w, a_mine], zp)
+        if kind == "A5":
+            return rc(kind, w, fin.at[w, a_mine], fin.at[w, a_mine], yp)
+        if kind == "B1":
+            return rc(kind, w, x_buf.at[w, b_all], rb1.at[s], zp)
+        if kind == "B2":
+            return rc(kind, w, x_buf.at[w, b_other], rb2.at[s], zm)
+        if kind == "B3":
+            return rc(kind, w, x_buf.at[w, b_mine], rb3.at[s], yp)
+        if kind == "B4":
+            return rc(kind, w, fin.at[w, b_mine], fin.at[w, b_mine], zm)
+        if kind == "B5a":
+            return rc(kind, w, fin.at[w, b_mine], fin.at[w, b_mine], zp)
+        if kind == "B5b":
+            return rc(kind, w, fin.at[w, b_other], fin.at[w, b_other], zp)
+        if kind == "G":
+            there = red.at[w, pl.ds(pl.multiple_of(c * RW, RW), RW)]
+            return rc(kind, w, fin.at[w], there, sib)
+
+    def p_ff(w):
+        return rc("P", w, ffg.at[w, pl.ds(pl.multiple_of((1 - c) * RW, RW), RW)], x_buf.at[w], sib)
+
+    def p_at(j):
+        return rc("P", n_ff + j, ag.at[2 * j + 1 - c], x_buf.at[n_ff + j], sib)
+
+    def local(w):
+        here = red.at[w, pl.ds(pl.multiple_of(c * RW, RW), RW)]
+        return pltpu.make_async_copy(fin.at[w], here, loc_sem.at[w])
+
+    def own_copy(w):
+        return pltpu.make_async_copy(
+            ffg.at[w, pl.ds(pl.multiple_of(c * RW, RW), RW)], own.at[lax.rem(w, 2)], own_sem.at[lax.rem(w, 2)]
+        )
+
+    def add(a, b):
+        return (a.astype(f32) + b.astype(f32)).astype(bf16)
+
+    def stage(s, t):
+        w = t - (s - 1)
+        ok = jnp.logical_and(w >= 0, w < waves)
+        slot = lax.rem(w, NS)
+        if s == 1:
+
+            @pl.when(jnp.logical_and(ok, w < n_ff))
+            def _():
+                @pl.when(w + 1 < n_ff)
+                def _():
+                    own_copy(w + 1).start()
+
+                p_ff(w).wait_recv()
+                own_copy(w).wait()
+                x_buf[w] = add(x_buf[w], own[lax.rem(w, 2)])
+
+            @pl.when(jnp.logical_and(ok, w >= n_ff))
+            def _():
+                p_at(w - n_ff).wait_recv()
+                x_buf[w] = add(x_buf[w], ag[2 * (w - n_ff) + c])
+
+            @pl.when(ok)
+            def _():
+                cp("A1", w).start()
+
+                @pl.when(outer)
+                def _():
+                    cp("B1", w).start()
+
+        if s == 2:
+
+            @pl.when(ok)
+            def _():
+                cp("A1", w).wait_recv()
+                x_buf[w, a_mine] = add(x_buf[w, a_mine], ra1[slot])
+
+                @pl.when(outer)
+                def _():
+                    cp("A2", w).start()
+
+                @pl.when(inner)
+                def _():
+                    cp("B1", w).wait_recv()
+                    x_buf[w, b_all] = add(x_buf[w, b_all], rb1[slot])
+                    cp("B2", w).start()
+
+        if s == 3:
+
+            @pl.when(jnp.logical_and(ok, inner))
+            def _():
+                cp("A2", w).wait_recv()
+                x_buf[w, a_mine] = add(x_buf[w, a_mine], ra2[slot])
+                cp("A3", w).start()
+                cp("B2", w).wait_recv()
+                x_buf[w, b_mine] = add(x_buf[w, b_mine], rb2[slot])
+                cp("B3", w).start()
+
+        if s == 4:
+
+            @pl.when(jnp.logical_and(ok, inner))
+            def _():
+                cp("A3", w).wait_recv()
+                fin[w, a_mine] = add(x_buf[w, a_mine], ra3[slot])
+                cp("A4", w).start()
+                cp("A5", w).start()
+                cp("B3", w).wait_recv()
+                fin[w, b_mine] = add(x_buf[w, b_mine], rb3[slot])
+                cp("B4", w).start()
+                cp("B5a", w).start()
+
+        if s == 5:
+
+            @pl.when(jnp.logical_and(ok, inner))
+            def _():
+                cp("B4", w).wait_recv()
+                cp("B5b", w).start()
+
+            @pl.when(jnp.logical_and(ok, outer))
+            def _():
+                cp("A4", w).wait_recv()
+                cp("A5", w).start()
+
+        if s == 6:
+
+            @pl.when(ok)
+            def _():
+                cp("A5", w).wait_recv()
+
+                @pl.when(outer)
+                def _():
+                    cp("B5a", w).wait_recv()
+                    cp("B5b", w).wait_recv()
+
+                cp("G", w).start()
+                local(w).start()
+
+
+    cos, sin = cs[0:8], cs[8:16]
+
+    def head(t):
+        qr = pl.ds(pl.multiple_of(t * 192, 64), 192)
+        vr = pl.ds(pl.multiple_of(t * 64, 64), 64)
+        qkv_s[...] = dot_nt(w_t[qr], h[...]) + bq[qr]
+        do_s[...] = dot_nt(wo[vr], g[...]).astype(bf16)
+        o, dq, dk, dv = attend_head(qkv_s[0:64], qkv_s[64:128], qkv_s[128:192], do_s[...], cos, sin)
+        att_t[vr] = o
+        dqkv_t[pl.ds(pl.multiple_of(t * 192, 64), 64)] = dq.astype(bf16)
+        dqkv_t[pl.ds(pl.multiple_of(t * 192 + 64, 64), 64)] = dk.astype(bf16)
+        dqkv_t[pl.ds(pl.multiple_of(t * 192 + 128, 64), 64)] = dv.astype(bf16)
+        ag[t, 0:192] = dot(dqkv_t[qr], h[...]).astype(bf16)
+        ag[t, 192:256] = dot(att_t[vr], g[...]).astype(bf16)
+
+    ch = 128
+    n_ch = out.shape[0] // ch
+
+    def xcopy(which, i):
+        src, dst = ((br_send, br_recv), (dh_send, dh_recv))[which]
+        r = pl.ds(pl.multiple_of(i * ch, ch), ch)
+        return pltpu.make_async_remote_copy(
+            src_ref=src.at[r], dst_ref=dst.at[r], send_sem=x_ss.at[which, i], recv_sem=x_rs.at[which, i],
+            device_id=xp, device_id_type=MESH,
+        )
+
+    def load(src, row, buf, sem):
+        k = pltpu.make_async_copy(src.at[pl.ds(row, ch)], buf, sem)
+        k.start()
+        k.wait()
+
+    def norm(i):
+        r = resid[i].astype(f32)
+        centered = r - jnp.mean(r, axis=1, keepdims=True)
+        inv = lax.rsqrt(jnp.mean(centered * centered, axis=1, keepdims=True) + epsilon)
+        return r, centered * inv, inv
+
+    def rows_of(who, i):
+        return pl.multiple_of(who * (n_ch * ch) + i * ch, ch)
+
+    def branch(row):
+        return dot(att_t[:, pl.ds(row, ch)].T, wo[...])
+
+    def back(row):
+        return dot(dqkv_t[:, pl.ds(row, ch)].T, w_t[...])
+
+    def add_sums(d, row):
+        _, normed, _ = norm(pl.ds(row, ch))
+        sums[0:1] = sums[0:1] + jnp.sum(d * normed, axis=0, keepdims=True)
+        sums[1:2] = sums[1:2] + jnp.sum(d, axis=0, keepdims=True)
+
+    def branch_far(i, _):
+        row = rows_of(1 - x, i)
+        load(ffb, row, ff_buf, ff_sem.at[0])
+        br_send[pl.ds(pl.multiple_of(i * ch, ch), ch)] = (branch(row) + ff_buf[...]).astype(bf16)
+        xcopy(0, i).start()
+        return 0
+
+    def back_far(i, _):
+        row = rows_of(1 - x, i)
+        load(ffd, row, ff_buf, ff_sem.at[0])
+        d = back(row) + ff_buf[...]
+        add_sums(d, row)
+        dh_send[pl.ds(pl.multiple_of(i * ch, ch), ch)] = d.astype(bf16)
+        xcopy(1, i).start()
+        return 0
+
+    def back_near(i, _):
+        row = rows_of(x, i)
+        load(ffd, row, ff_buf, ff_sem.at[0])
+        d = back(row) + ff_buf[...]
+        add_sums(d, row)
+        dh_own[pl.ds(pl.multiple_of(i * ch, ch), ch)] = d
+        return 0
+
+    def branch_near(i, _):
+        row = rows_of(x, i)
+        here = pl.ds(pl.multiple_of(i * ch, ch), ch)
+        load(ffb, row, ff_buf, ff_sem.at[0])
+        xcopy(0, i).wait_recv()
+        total = branch(row) + ff_buf[...] + br_recv[here].astype(f32)
+        out[here] = (resid[pl.ds(row, ch)].astype(f32) + total + vecs[1:2]).astype(bf16)
+        return 0
+
+    def finish(i, _):
+        row = rows_of(x, i)
+        here = pl.ds(pl.multiple_of(i * ch, ch), ch)
+        xcopy(1, i).wait_recv()
+        _, normed, inv = norm(pl.ds(row, ch))
+        d_hat = (dh_own[here] + dh_recv[here].astype(f32)) * vecs[0:1]
+        first = jnp.mean(d_hat, axis=1, keepdims=True)
+        second = jnp.mean(d_hat * normed, axis=1, keepdims=True)
+        grad_in[here] = g[pl.ds(row, ch)].astype(f32) + inv * (d_hat - first - normed * second)
+        return 0
+
+    def small(i):
+        device = (sib, yp, zp, zm, xp)[i]
+        return pltpu.make_async_remote_copy(
+            src_ref=sm_send.at[i], dst_ref=sm_recv.at[i], send_sem=sm_ss.at[i], recv_sem=sm_rs.at[i],
+            device_id=device, device_id_type=MESH,
+        )
+
+
+    def start_ff(w, _):
+        p_ff(w).start()
+        return 0
+
+    own_copy(0).start()
+    lax.fori_loop(0, n_ff, start_ff, 0)
+    sums[...] = jnp.zeros_like(sums)
+
+    def tick(t, _):
+        for s in range(1, 7):
+            stage(s, t)
+
+        @pl.when(t < heads)
+        def _():
+            head(t)
+
+            @pl.when(lax.rem(t, 2) == 1)
+            def _():
+                p_at(t // 2).start()
+
+        at = lambda k: pl.when(t == heads + k)
+
+        @at(0)
+        def _():
+            lax.fori_loop(0, n_ch, branch_far, 0)
+
+        @at(1)
+        def _():
+            lax.fori_loop(0, n_ch, back_far, 0)
+
+        @at(2)
+        def _():
+            lax.fori_loop(0, n_ch, back_near, 0)
+            ones = jnp.ones((8, dqkv_t.shape[1]), bf16)
+            bias = dot_nt(ones, dqkv_t[...])
+            sm_send[0] = small_in[...]
+            wide = small_in.shape[1]
+            sm_send[0, 3:4] = bias[0:1, :wide]
+            sm_send[0, 4:5, 0 : bias.shape[1] - wide] = bias[0:1, wide:]
+            sm_send[0, 5:7] = sums[0:2]
+            small(0).start()
+
+        @at(3)
+        def _():
+            lax.fori_loop(0, n_ch, branch_near, 0)
+
+        for k in range(1, 6):
+
+            @at(2 + k)
+            def _():
+                small(k - 1).wait_recv()
+                total = sm_send[k - 1] + sm_recv[k - 1]
+                if k < 4:
+                    sm_send[k] = total
+                    small(k).start()
+                elif k == 4:
+                    small_out[...] = total
+                    sm_send[4] = total
+                    small(4).start()
+                else:
+                    small_out[5:7] = total[5:7]
+
+        @at(8)
+        def _():
+            lax.fori_loop(0, n_ch, finish, 0)
+
+        return 0
+
+    lax.fori_loop(0, waves + 5, tick, 0)
+
+    def drain(w, _):
+        cp("A1", w).wait_send()
+        cp("A5", w).wait_send()
+        cp("G", w).wait()
+        local(w).wait()
+
+        @pl.when(outer)
+        def _():
+            cp("B1", w).wait_send()
+            cp("A2", w).wait_send()
+
+        @pl.when(inner)
+        def _():
+            for k in ("B2", "A3", "B3", "A4", "B4", "B5a", "B5b"):
+                cp(k, w).wait_send()
+
+        @pl.when(w < n_ff)
+        def _():
+            p_ff(w).wait_send()
+
+        @pl.when(w >= n_ff)
+        def _():
+            p_at(w - n_ff).wait_send()
+
+        return 0
+
+    lax.fori_loop(0, waves, drain, 0)
+
+    def drain_x(i, _):
+        xcopy(0, i).wait_send()
+        xcopy(1, i).wait_send()
+        return 0
+
+    lax.fori_loop(0, n_ch, drain_x, 0)
+    for i in range(5):
+        small(i).wait_send()
+
+
+def mega(ffg, h, g, w_t, bq, wo, cs, ffb, ffd, resid, vecs, small_in):
+    rows, width = h.shape
+    heads = wo.shape[0] // HD
+    n_ff = ffg.shape[0]
+    waves = n_ff + heads // 2
+    half = rows // 2
+    n_ch = half // 128
+    vm = pl.BlockSpec(memory_space=pltpu.VMEM)
+    hbm = pl.BlockSpec(memory_space=pl.ANY)
+    dma = pltpu.SemaphoreType.DMA
+    return pl.pallas_call(
+        functools.partial(mega_kernel, n_ff, heads),
+        in_specs=[hbm, vm, vm, vm, vm, vm, vm, hbm, hbm, vm, vm, vm],
+        out_specs=[hbm, vm, vm, vm],
+        out_shape=[
+            jax.ShapeDtypeStruct((waves, 2 * RW, width), bf16),
+            jax.ShapeDtypeStruct((half, width), bf16),
+            jax.ShapeDtypeStruct((half, width), f32),
+            jax.ShapeDtypeStruct((8, width), f32),
+        ],
+        scratch_shapes=[
+            pltpu.VMEM((waves, RW, width), bf16),
+            pltpu.VMEM((2, RW, width), bf16),
+            pltpu.VMEM((heads, RW, width), bf16),
+            pltpu.VMEM((waves, RW, width), bf16),
+            pltpu.VMEM((NS, RQ, width), bf16),
+            pltpu.VMEM((NS, RQ, width), bf16),
+            pltpu.VMEM((NS, RQ, width), bf16),
+            pltpu.VMEM((NS, 2 * RQ, width), bf16),
+            pltpu.VMEM((NS, RQ, width), bf16),
+            pltpu.VMEM((NS, RQ, width), bf16),
+            pltpu.VMEM((3 * HD, rows), f32),
+            pltpu.VMEM((HD, rows), bf16),
+            pltpu.VMEM((heads * 3 * HD, rows), bf16),
+            pltpu.VMEM((heads * HD, rows), bf16),
+            pltpu.VMEM((half, width), f32),
+            pltpu.VMEM((half, width), bf16),
+            pltpu.VMEM((half, width), bf16),
+            pltpu.VMEM((half, width), bf16),
+            pltpu.VMEM((half, width), bf16),
+            pltpu.VMEM((128, width), f32),
+            pltpu.VMEM((8, width), f32),
+            pltpu.VMEM((5, 8, width), f32),
+            pltpu.VMEM((5, 8, width), f32),
+            pltpu.VMEM((8, width), f32),
+            dma((len(KINDS), waves)),
+            dma((len(KINDS), waves)),
+            dma((2,)),
+            dma((waves,)),
+            dma((2, n_ch)),
+            dma((2, n_ch)),
+            dma((2,)),
+            dma((5,)),
+            dma((5,)),
+            dma((2,)),
+        ],
+        compiler_params=pltpu.CompilerParams(collective_id=0, has_side_effects=True, vmem_limit_bytes=62 * 2**20),
+        name="attention_and_sums",
+    )(ffg, h, g, w_t, bq, wo, cs, ffb, ffd, resid, vecs, small_in)
+
+
+def shards(residual, ln_gain, ln_bias, w_qkv, b_qkv, w_out, b_out, w_up, b_up, w_down, b_down, grad_out):
+    x = lax.axis_index("tensor")
+    swap = [(0, 1), (1, 0)]
+    far_resid = lax.ppermute(residual, "tensor", swap)
+    grad_first, far_resid = lax.optimization_barrier((grad_out, far_resid))
+    far_grad = lax.ppermute(grad_first, "tensor", swap)
+
+    def group(near, far):
+        return jnp.where(x == 0, jnp.concatenate([near, far]), jnp.concatenate([far, near]))
+
+    resid = group(residual, far_resid)
+    wide = resid.astype(f32)
+    centered = wide - jnp.mean(wide, axis=1, keepdims=True)
+    variance = jnp.mean(centered * centered, axis=1, keepdims=True)
+    normed = centered * lax.rsqrt(variance + epsilon)
+    h = (normed * ln_gain + ln_bias).astype(bf16)
+    g = group(grad_out, far_grad)
+    up_lin = dot(h, w_up) + b_up
+    act_wide, gelu_back = jax.vjp(functools.partial(jax.nn.gelu, approximate=False), up_lin)
+    slope = gelu_back(jnp.ones_like(up_lin))[0].astype(bf16)
+    act = act_wide.astype(bf16)
+    act, slope = lax.optimization_barrier((act, slope))
+    ffb = dot(act, w_down)
+    d_up = (dot_nt(g, w_down) * slope.astype(f32)).astype(bf16)
+    ffd = dot_nt(d_up, w_up)
+    g_down = dot_tn(act, g).astype(bf16)
+    g_up = dot_tn(h, d_up).astype(bf16)
+    rows, width = h.shape
+    n_up = g_up.shape[1] // width
+    blocks = [g_down.reshape(-1, 2 * RW, width)]
+    blocks += [g_up[:, i * width : (i + 1) * width].reshape(-1, 2 * RW, width) for i in range(n_up)]
+    ffg = jnp.concatenate(blocks)
+    n_down = blocks[0].shape[0]
+    gb_up = jnp.sum(d_up, axis=0, dtype=f32)
+    gb_near = jnp.sum(grad_out, axis=0, dtype=f32)
+    gb_far = jnp.sum(far_grad, axis=0, dtype=f32)
+    gb_out = gb_near + gb_far
+    small_in = jnp.concatenate([gb_up.reshape(n_up, width), gb_out[None], jnp.zeros((7 - n_up, width), f32)])
+    cosine, sine = turn_tables(rows)
+    cs = jnp.concatenate([cosine.T, sine.T])
+    vecs = jnp.concatenate([ln_gain[None], (b_out + b_down)[None], jnp.zeros((6, width), f32)])
+    red, out, grad_in, small = mega(ffg, h, g, w_qkv.T, b_qkv[:, None], w_out, cs, ffb, ffd, resid, vecs, small_in)
+    grad_w_down = red[:n_down].reshape(-1, width).astype(f32)
+    per = width // (2 * RW)
+    ups = [red[n_down + i * per : n_down + (i + 1) * per].reshape(width, width) for i in range(n_up)]
+    grad_w_up = jnp.concatenate(ups, axis=1).astype(f32)
+    at = red[n_down + n_up * per :].reshape(-1, RW, width)
+    grad_w_qkv = at[:, : 3 * HD].reshape(-1, width).T.astype(f32)
+    grad_w_out = at[:, 3 * HD :].reshape(-1, width).astype(f32)
+    gb_up = small[:n_up].reshape(-1)
+    gb_out = small[2]
+    gb_qkv = small[3:5].reshape(-1)[: b_qkv.shape[0]]
+    return out, grad_in, small[5], small[6], grad_w_qkv, gb_qkv, grad_w_out, gb_out, grad_w_up, gb_up, grad_w_down, gb_out
 
 
 def contract_rows(left, right):
@@ -24,15 +605,6 @@
     return lax.dot_general(
         left, right, (((1,), (1,)), ((), ())), preferred_element_type=jnp.float32
     )
-
-
-def turn_tables(seqlen):
-    half_rot = ROT // 2
-    exponent = jnp.arange(half_rot, dtype=jnp.float32) * (2.0 / ROT)
-    inverse = 1.0 / 10000.0**exponent
-    places = jnp.arange(seqlen, dtype=jnp.float32)
-    angles = places[:, None] * inverse[None, :]
-    return (jnp.cos(angles), jnp.sin(angles))
 
 
 def turn_heads(heads, cosine, sine):
@@ -59,7 +631,7 @@
     )
 
 
-def shards(
+def shards_any(
     residual, ln_gain, ln_bias, w_qkv, b_qkv, w_out, b_out, w_up, b_up, w_down, b_down, grad_out
 ):
     rows_here = residual.shape[0]
@@ -78,7 +650,7 @@
     seq_count = group_rows // seqlen
     qkv = jnp.dot(h_full, w_qkv, preferred_element_type=jnp.float32) + b_qkv
     up_lin = jnp.dot(h_full, w_up, preferred_element_type=jnp.float32) + b_up
-    act_wide, gelu_back = jax.vjp(partial(jax.nn.gelu, approximate=False), up_lin)
+    act_wide, gelu_back = jax.vjp(functools.partial(jax.nn.gelu, approximate=False), up_lin)
     act = act_wide.astype(jnp.bfloat16)
     cosine, sine = turn_tables(seqlen)
     causal = jnp.arange(seqlen)[:, None] >= jnp.arange(seqlen)[None, :]
@@ -195,8 +767,9 @@
 
 
 def solution(mesh):
+    small_slice = mesh.shape["dp"] == 16 and mesh.shape["tensor"] == 2
     return jax.shard_map(
-        shards,
+        shards if small_slice else shards_any,
         mesh=mesh,
         in_specs=(
             P(("dp", "tensor"), None),

time: 842 us -> 302 us (0.36); the launches traced: 832 us -> 301 us
  waiting for transfers between devices: 417 us -> 13.7 us
  Pallas kernels: 0 us -> 152 us
  matrix products: 183 us -> 58.7 us
  blocking collectives: 100 us -> 0 us
  other arithmetic: 77.5 us -> 39.1 us
  between operations: 14.7 us -> 0.86 us
    psum x1 -> x0, waiting for transfers between devices: 383 us -> none  [shards(): lax.psum((grad_w_qkv, grad_b_qkv, grad_w_out, grad_w_up, grad_b_up, grad_...]
    pallas_call x0 -> x1, Pallas kernels: none -> 152 us  [mega(): pl.pallas_call(functools.partial(mega_kernel, n_ff, heads), in_specs=[hbm...]
    dot_general x18 -> x6, matrix products: 183 us -> 58.7 us  [the longest x2 32.7 us: dot(): lax.dot_general(left, right, (((1,), (0,)), ((), ())), preferred_element_...]
    psum x2 -> x0, blocking collectives: 100 us -> none  [the longest x1 61.4 us: shards(): lax.psum((grad_w_qkv, grad_b_qkv, grad_w_out, grad_w_up, grad_b_up, grad_...]
    all_gather x2 -> x0, waiting for transfers between devices: 33.7 us -> none  [the longest x1 33.6 us: shards(): h_full = lax.all_gather(h_local, 'tensor', axis=0, tiled=True)]
    reduce_sum x5 -> x3, other arithmetic: 23.1 us -> 3.66 us  [the longest x1 1.41 us: shards(): gb_far = jnp.sum(far_grad, axis=0, dtype=f32)]
    convert_element_type x3 -> x6, other arithmetic: 41.5 us -> 25.3 us  [the longest x1 7.98 us: shards(): act = act_wide.astype(bf16)]
    ppermute x0 -> x2, waiting for transfers between devices: none -> 13.7 us  [the longest x1 13.7 us: shards(): far_resid = lax.ppermute(residual, 'tensor', swap)]
  transfers between devices with their start and end apart: 5 -> 2, of which waited for: 2 -> 1; matrix products, arithmetic and copies ran while one was open for 15% -> 17% of each run, Pallas kernels for 0% -> 0%
where the time goes in v1:
time: 302 us; the launch traced here: 301 us
  Pallas kernels  152 us (50%)
  matrix products  58.7 us (19%)
  other arithmetic  39.1 us (13%)
  local copies, waits for them, and re-layouts  31.9 us (11%)
  waiting for transfers between devices  13.7 us (5%)
  starting transfers between devices  4.81 us (2%)
    pallas_call x1, Pallas kernels, mega(): pl.pallas_call(functools.partial(mega_kernel, n_ff, heads), in_specs=[hbm...  152 us
    dot_general x2, matrix products, dot(): lax.dot_general(left, right, (((1,), (0,)), ((), ())), preferred_element_...  32.7 us
    unnamed x40, local copies, waits for them, and re-layouts  15 us
    ppermute x1, waiting for transfers between devices, shards(): far_resid = lax.ppermute(residual, 'tensor', swap)  13.7 us
    dot_general x2, matrix products, dot_nt(): lax.dot_general(left, right, (((1,), (1,)), ((), ())), preferred_element_...  13.6 us
    dot_general x2, matrix products, dot_tn(): lax.dot_general(left, right, (((0,), (0,)), ((), ())), preferred_element_...  12.4 us
    convert_element_type x1, other arithmetic, shards(): act = act_wide.astype(bf16)  7.98 us
    convert_element_type x1, other arithmetic, shards(): grad_w_down = red[:n_down].reshape(-1, width).astype(f32)  6.78 us
  transfers between devices with their start and end apart: 2, of which 1 were waited for; matrix products, arithmetic and copies ran while one was open for 17% of the time, Pallas kernels for 0%

profile of v1, /device:TPU:0, one launch (start us, length us, event | category | flops | bytes accessed | tf_op | source)
XLA Modules:
  0.0 301.2 jit_solution(10730293789576598373)
XLA Ops:
  0.6 0.0 copy-start.12
  0.7 0.0 copy-start.11
  0.7 0.0 copy-start.9
  0.7 3.0 collective-permute-start
  3.7 0.1 pad.7.clone
  3.8 0.1 pad.4.clone
  3.8 1.9 broadcast_in_dim.28.bq
  5.8 4.7 %copy.26 = bf16[1024,1536]{0,1:T(8,128)(2,1)} copy(bf16[1024,1536]{1,0:T(8,128)(2,1)} %param.15) | data formatting | bytes 6291456 | tf_op args[3]
  10.4 0.0 copy-done.12
  10.4 0.0 copy-done.11
  10.5 0.2 fusion.13
  10.7 0.6 pad_maximum_fusion.1.cs
  11.3 1.4 convert_reduce_fusion.3
  12.7 0.0 copy-done.9
  12.7 0.7 maximum_maximum_fusion.vecs
  13.4 13.7 %collective-permute-done = bf16[512,1024]{1,0:T(8,128)(2,1)S(1)} collective-permute-done((bf16[512,1024]{1,0:T(8,128)(2,1)}, bf16[512,1024]{1,0:T(8,128)(2,1)S(1)}, u32[]{:S(2)}, u32[]{:S(2)}) %collective-permute-start) | collective-permute-done | bytes 1048608 | tf_op jit(solution)/shard_map/ppermute | solution.py:546
  27.0 0.0 copy-done.6
  27.1 0.8 convert_reduce_fusion.1
  27.9 0.0 copy-start
  27.9 0.0 copy-start.10
  27.9 0.0 copy-start.15
  28.0 0.7 fusion.8
  28.7 1.8 collective-permute-start.1
  30.5 0.0 copy-done
  30.5 0.0 copy-done.13
  30.5 0.8 fusion.11.h
  31.3 0.0 copy-done.10
  31.3 0.0 copy-start.1
  31.3 24.4 %add_convert_fusion = (bf16[1024,2048]{1,0:T(8,128)(2,1)}, f32[1024,2048]{1,0:T(8,128)}, f32[1024,2048]{1,0:T(8,128)}) fusion(f32[2048]{0:T(1024)S(1)} %copy-done.10, bf16[1024,1024]{1,0:T(8,128)(2,1)S(1)} %fusion.11.h, bf16[1024,2048]{1,0:T(8,128)(2,1)S(1)} %copy-done.15), kind=kOutput, calls=%fused_computation.5 | convolution fusion | flops 4441767936 | bytes 27271168 | tf_op jit(solution)/shard_map/dot_general | solution.py:21
  55.8 8.0 %multiply_convert_fusion.1 = bf16[1024,2048]{1,0:T(8,128)(2,1)S(1)} fusion(f32[1024,2048]{1,0:T(8,128)} %get-tuple-element.41, f32[1024,2048]{1,0:T(8,128)} %get-tuple-element.57, f32[2048]{0:T(1024)S(1)} %copy-done.10), kind=kLoop, calls=%fused_computation.6 | loop fusion | flops 8388608 | bytes 20979712 | tf_op jit(solution)/shard_map/convert_element_type | solution.py:563
  63.7 8.2 %fusion.19.ffb = f32[1024,1024]{1,0:T(8,128)} fusion(bf16[1024,2048]{1,0:T(8,128)(2,1)S(1)} %multiply_convert_fusion.1, bf16[2048,1024]{1,0:T(8,128)(2,1)} %param.21), kind=kOutput, calls=%fused_computation.55 | convolution fusion | flops 4294967296 | bytes 12582912 | tf_op jit(solution)/shard_map/dot_general | solution.py:21
  72.0 0.0 collective-permute-done.1
  72.0 3.4 %maximum_select_fusion.1.g = bf16[1024,1024]{1,0:T(8,128)(2,1)S(1)} fusion(bf16[512,1024]{1,0:T(8,128)(2,1)} %collective-permute-done.1, bf16[512,1024]{1,0:T(8,128)(2,1)} %param.23, pred[]{:T(512)S(6)} %eq.4), kind=kLoop, calls=%fused_computation.34 | loop fusion | flops 9437184 | bytes 4194305 | tf_op jit(solution)/shard_map/jit(_where)/select_n | solution.py:551
  75.4 0.0 copy-done.14
  75.4 0.0 copy-start.16
  75.4 7.5 %convert_reduce_fusion = (f32[2048]{0:T(1024)S(1)}, bf16[1024,2048]{1,0:T(8,128)(2,1)S(1)}) fusion(bf16[1024,2048]{1,0:T(8,128)(2,1)} %get-tuple-element.23, bf16[1024,1024]{1,0:T(8,128)(2,1)S(1)} %maximum_select_fusion.1.g, bf16[2048,1024]{1,0:T(8,128)(2,1)S(1)} %copy-done.14), kind=kOutput, calls=%fused_computation.3 | convolution fusion | flops 4305451008 | bytes 14688256 | tf_op jit(solution)/shard_map/dot_general | solution.py:25
  82.9 6.1 %fusion.20.ffd = f32[1024,1024]{1,0:T(8,128)} fusion(bf16[1024,2048]{1,0:T(8,128)(2,1)S(1)} %get-tuple-element.59, bf16[1024,2048]{1,0:T(8,128)(2,1)S(1)} %copy-done.16), kind=kOutput, calls=%fused_computation.56 | convolution fusion | flops 4294967296 | bytes 12582912 | tf_op jit(solution)/shard_map/dot_general | solution.py:25
  89.0 0.0 copy-done.1
  89.0 6.2 %convolution_convert_fusion = bf16[1024,2048]{1,0:T(8,128)(2,1)} fusion(bf16[1024,1024]{1,0:T(8,128)(2,1)S(1)} %fusion.11.h, bf16[1024,2048]{1,0:T(8,128)(2,1)S(1)} %get-tuple-element.59), kind=kOutput, calls=%fused_computation.31 | convolution fusion | flops 4297064448 | bytes 10485760 | tf_op jit(solution)/shard_map/dot_general | solution.py:29
  95.2 0.0 copy-done.2
  95.2 6.2 %convolution_convert_fusion.1 = bf16[2048,1024]{1,0:T(8,128)(2,1)} fusion(bf16[1024,2048]{1,0:T(8,128)(2,1)S(1)} %multiply_convert_fusion.1, bf16[1024,1024]{1,0:T(8,128)(2,1)S(1)} %maximum_select_fusion.1.g), kind=kOutput, calls=%fused_computation.32 | convolution fusion | flops 4297064448 | bytes 10485760 | tf_op jit(solution)/shard_map/dot_general | solution.py:29
  101.5 2.8 fusion.17
  104.3 1.4 convert_reduce_fusion.2
  105.7 0.7 maximum_maximum_fusion.1.small_in
  106.4 3.8 %pad_maximum_fusion.ffg = bf16[8,512,1024]{2,1,0:T(8,128)(2,1)} fusion(bf16[2,512,1024]{2,1,0:T(8,128)(2,1)S(1)} %bitcast.51, bf16[2,512,1024]{2,1,0:T(8,128)(2,1)S(1)} %bitcast.50, bf16[4,512,1024]{2,1,0:T(8,128)(2,1)S(1)} %bitcast.52), kind=kLoop, calls=%fused_computation.2 | loop fusion | flops 8388608 | bytes 16777216 | tf_op jit(solution)/shard_map/concatenate | solution.py:574
  110.2 152.3 %attention_and_sums.1 = (bf16[12,512,1024]{2,1,0:T(8,128)(2,1)}, bf16[512,1024]{1,0:T(8,128)(2,1)}, f32[512,1024]{1,0:T(8,128)}, f32[8,1024]{1,0:T(8,128)}) custom-call(bf16[8,512,1024]{2,1,0:T(8,128)(2,1)} %pad_maximum_fusion.ffg, bf16[1024,1024]{1,0:T(8,128)(2,1)} %copy-done.1, bf16[1024,1024]{1,0:T(8,128)(2,1)} %copy-done.2, bf16[1536,1024]{1,0:T(8,128)(2,1)} %bitcast.47, ...), custom_call_target="tpu_custom_call" | custom-call | tf_op jit(solution)/shard_map/attention_and_sums/pallas_call | solution.py:492
  262.5 1.5 fusion.18
  264.0 0.8 slice_bitcast_fusion
  264.8 4.2 %fusion.16 = (bf16[2,512,1024]{2,1,0:T(8,128)(2,1)S(1)}, bf16[2,512,1024]{2,1,0:T(8,128)(2,1)}) fusion(bf16[12,512,1024]{2,1,0:T(8,128)(2,1)} %get-tuple-element.27), kind=kLoop, calls=%fused_computation.52 | loop fusion | bytes 8388608 | tf_op jit(solution)/shard_map/slice | solution.py:587
  269.0 5.2 %fusion.15 = (bf16[4,512,1024]{2,1,0:T(8,128)(2,1)}, bf16[4,512,1024]{2,1,0:T(8,128)(2,1)S(1)}) fusion(bf16[12,512,1024]{2,1,0:T(8,128)(2,1)} %get-tuple-element.27), kind=kLoop, calls=%fused_computation.51 | loop fusion | bytes 16777216 | tf_op jit(solution)/shard_map/slice | solution.py:585
  274.3 0.1 slice.60
  274.3 0.3 slice.58
  274.7 1.6 bitcast_convert_fusion.1
  276.3 3.7 %convert_bitcast_fusion = f32[1024,1536]{0,1:T(8,128)} fusion(bf16[8,192,1024]{2,1,0:T(8,128)(2,1)S(1)} %slice.58), kind=kLoop, calls=%fused_computation.20 | loop fusion | flops 1572864 | bytes 9437184 | tf_op jit(solution)/shard_map/convert_element_type | solution.py:590
  279.9 6.6 %copy.28 = f32[1024,1536]{1,0:T(8,128)} copy(f32[1024,1536]{0,1:T(8,128)} %convert_bitcast_fusion) | data formatting | bytes 12582912
  286.5 6.8 %bitcast_convert_fusion = f32[2048,1024]{1,0:T(8,128)} fusion(bf16[4,512,1024]{2,1,0:T(8,128)(2,1)} %get-tuple-element.44), kind=kLoop, calls=%fused_computation.30 | loop fusion | flops 2097152 | bytes 12582912 | tf_op jit(solution)/shard_map/convert_element_type | solution.py:585
  293.3 0.6 copy_bitcast_fusion
  293.9 0.0 copy-done.3
  293.9 4.4 %maximum_convert_fusion = f32[1024,2048]{1,0:T(8,128)} fusion(bf16[1024,1024]{1,0:T(8,128)(2,1)S(1)} %bitcast.49, bf16[1024,1024]{1,0:T(8,128)(2,1)S(1)} %bitcast.48), kind=kLoop, calls=%fused_computation.29 | loop fusion | flops 8388608 | bytes 12582912 | tf_op jit(solution)/shard_map/convert_element_type | solution.py:588
  298.3 0.0 copy-done.8
  298.3 0.6 copy.36
  298.9 1.0 copy.37
  299.9 0.0 copy-done.5
  299.9 1.3 copy.38
  (21 shorter events, 0.1 us)
Async XLA Ops:
  0.6 9.8 %copy-start.12 = (f32[1024]{0:T(1024)S(1)}, f32[1024]{0:T(1024)}, u32[]{:S(2)}) copy-start(f32[1024]{0:T(1024)} %param.22) | copy-start | bytes 12292
  0.7 9.8 %copy-start.11 = (f32[1024]{0:T(1024)S(1)}, f32[1024]{0:T(1024)}, u32[]{:S(2)}) copy-start(f32[1024]{0:T(1024)} %param.18) | copy-start | bytes 12292
  0.7 12.1 %copy-start.9 = (f32[1024]{0:T(1024)S(1)}, f32[1024]{0:T(1024)}, u32[]{:S(2)}) copy-start(f32[1024]{0:T(1024)} %param.13) | copy-start | bytes 12292
  0.7 26.4 %collective-permute-start = (bf16[512,1024]{1,0:T(8,128)(2,1)}, bf16[512,1024]{1,0:T(8,128)(2,1)S(1)}, u32[]{:S(2)}, u32[]{:S(2)}) collective-permute-start(bf16[512,1024]{1,0:T(8,128)(2,1)} %param.12), channel_id=1, source_target_pairs={{0,1},{1,0},{2,3},{3,2},{4,5},{5,4},{6,7},{7,6},{8,9},{9,8},{10,11... | collective-permute-start | bytes 3145736 | tf_op jit(solution)/shard_map/ppermute | solution.py:546
  3.8 23.2 %copy-start.6 = (bf16[512,1024]{1,0:T(8,128)(2,1)S(1)}, bf16[512,1024]{1,0:T(8,128)(2,1)}, u32[]{:S(2)}) copy-start(bf16[512,1024]{1,0:T(8,128)(2,1)} %param.12) | copy-start | bytes 3145732
  10.4 20.0 %copy-start.13 = (f32[1024]{0:T(1024)S(1)}, f32[1024]{0:T(1024)}, u32[]{:S(2)}) copy-start(f32[1024]{0:T(1024)} %param.14) | copy-start | bytes 12292
  27.9 2.6 copy-start
  27.9 3.4 %copy-start.10 = (f32[2048]{0:T(1024)S(1)}, f32[2048]{0:T(1024)}, u32[]{:S(2)}) copy-start(f32[2048]{0:T(1024)} %param.20) | copy-start | bytes 24580
  27.9 3.4 %copy-start.15 = (bf16[1024,2048]{1,0:T(8,128)(2,1)S(1)}, bf16[1024,2048]{1,0:T(8,128)(2,1)}, u32[]{:S(2)}) copy-start(bf16[1024,2048]{1,0:T(8,128)(2,1)} %param.19) | copy-start | bytes 12582916
  28.7 43.3 %collective-permute-start.1 = (bf16[512,1024]{1,0:T(8,128)(2,1)}, bf16[512,1024]{1,0:T(8,128)(2,1)}, u32[]{:S(2)}, u32[]{:S(2)}) collective-permute-start(bf16[512,1024]{1,0:T(8,128)(2,1)} %param.23), channel_id=1, source_target_pairs={{0,1},{1,0},{2,3},{3,2},{4,5},{5,4},{6,7},{7,6},{8,9},{9,8},{10,11... | collective-permute-start | bytes 3145736 | tf_op jit(solution)/shard_map/ppermute | solution.py:548
  31.3 57.7 %copy-start.1 = (bf16[1024,1024]{1,0:T(8,128)(2,1)}, bf16[1024,1024]{1,0:T(8,128)(2,1)S(1)}, u32[]{:S(2)}) copy-start(bf16[1024,1024]{1,0:T(8,128)(2,1)S(1)} %fusion.11.h) | copy-start | bytes 6291460
  72.0 3.4 %copy-start.14 = (bf16[2048,1024]{1,0:T(8,128)(2,1)S(1)}, bf16[2048,1024]{1,0:T(8,128)(2,1)}, u32[]{:S(2)}) copy-start(bf16[2048,1024]{1,0:T(8,128)(2,1)} %param.21) | copy-start | bytes 12582916
  75.4 19.8 %copy-start.2 = (bf16[1024,1024]{1,0:T(8,128)(2,1)}, bf16[1024,1024]{1,0:T(8,128)(2,1)S(1)}, u32[]{:S(2)}) copy-start(bf16[1024,1024]{1,0:T(8,128)(2,1)S(1)} %maximum_select_fusion.1.g) | copy-start | bytes 6291460
  75.4 7.5 %copy-start.16 = (bf16[1024,2048]{1,0:T(8,128)(2,1)S(1)}, bf16[1024,2048]{1,0:T(8,128)(2,1)}, u32[]{:S(2)}) copy-start(bf16[1024,2048]{1,0:T(8,128)(2,1)} %param.19) | copy-start | bytes 12582916
  101.5 4.9 %copy-start.4 = (bf16[2048,1024]{1,0:T(8,128)(2,1)S(1)}, bf16[2048,1024]{1,0:T(8,128)(2,1)}, u32[]{:S(2)}) copy-start(bf16[2048,1024]{1,0:T(8,128)(2,1)} %convolution_convert_fusion.1) | copy-start | bytes 12582916
  264.0 34.3 %copy-start.8 = (f32[1,1024]{1,0:T(1,128)}, f32[1,1024]{1,0:T(1,128)S(1)}, u32[]{:S(2)}) copy-start(f32[1,1024]{1,0:T(1,128)S(1)} %get-tuple-element.52) | copy-start | bytes 12292
  286.5 7.4 %copy-start.3 = (bf16[2,512,1024]{2,1,0:T(8,128)(2,1)S(1)}, bf16[2,512,1024]{2,1,0:T(8,128)(2,1)}, u32[]{:S(2)}) copy-start(bf16[2,512,1024]{2,1,0:T(8,128)(2,1)} %get-tuple-element.47) | copy-start | bytes 6291460
  293.9 5.0 %copy-start.7 = (bf16[512,1024]{1,0:T(8,128)(2,1)S(1)}, bf16[512,1024]{1,0:T(8,128)(2,1)}, u32[]{:S(2)}) copy-start(bf16[512,1024]{1,0:T(8,128)(2,1)} %get-tuple-element.98) | copy-start | bytes 3145732
  293.9 6.0 %copy-start.5 = (f32[512,1024]{1,0:T(8,128)S(1)}, f32[512,1024]{1,0:T(8,128)}, u32[]{:S(2)}) copy-start(f32[512,1024]{1,0:T(8,128)} %get-tuple-element.99) | copy-start | bytes 6291460

commit v2 on v1

--- a/solution.py
+++ b/solution.py
@@ -25,10 +25,6 @@
     return lax.dot_general(left, right, (((1,), (1,)), ((), ())), preferred_element_type=f32)
 
 
-def dot_tn(left, right):
-    return lax.dot_general(left, right, (((0,), (0,)), ((), ())), preferred_element_type=f32)
-
-
 def turn_tables(seqlen):
     half_rot = ROT // 2
     exponent = jnp.arange(half_rot, dtype=f32) * (2.0 / ROT)
@@ -45,55 +41,84 @@
 
 def attend_head(q_t, k_t, v_t, do_t, cos, sin, blk=256):
     seq = q_t.shape[1]
+    nb = seq // blk
     qs = turn(q_t, cos, sin, 1.0).astype(bf16) * jnp.asarray(0.125, bf16)
     kb = turn(k_t, cos, sin, 1.0).astype(bf16)
     vb = v_t.astype(bf16)
     keys, values, queries, grads = kb.T, vb.T, qs.T, do_t.T
-    nb = seq // blk
-    outs, dqs = [], []
-    dv_sum, dk_sum = [None] * nb, [None] * nb
+    seen = lax.broadcasted_iota(jnp.int32, (blk, blk), 0) <= lax.broadcasted_iota(jnp.int32, (blk, blk), 1)
+    outs, dqs, dv_sum, dk_sum = [], [], [None] * nb, [None] * nb
+
+    def products(i):
+        kk, sl = (i + 1) * blk, slice(i * blk, (i + 1) * blk)
+        return dot(keys[:kk], qs[:, sl]), dot(values[:kk], do_t[:, sl])
+
+    def gather(sums, i, v):
+        for j in range(i + 1):
+            a = v[j * blk : (j + 1) * blk]
+            sums[j] = a if sums[j] is None else sums[j] + a
+
+    def back(i, p, dp):
+        kk, sl = (i + 1) * blk, slice(i * blk, (i + 1) * blk)
+        ds = (p * (dp - jnp.sum(p * dp, axis=0, keepdims=True))).astype(bf16)
+        dqs.append(dot(kb[:, :kk], ds) * 0.125)
+        gather(dk_sum, i, dot(ds, queries[sl]))
+
+    ahead, behind = products(0), None
     for i in range(nb):
         kk, sl = (i + 1) * blk, slice(i * blk, (i + 1) * blk)
-        s = dot(keys[:kk], qs[:, sl])
-        rows = lax.broadcasted_iota(jnp.int32, (blk, blk), 0)
-        cols = lax.broadcasted_iota(jnp.int32, (blk, blk), 1)
-        diag = jnp.where(rows <= cols, s[i * blk :], -1e30)
+        s, dp = ahead
+        if i + 1 < nb:
+            ahead = products(i + 1)
+        diag = jnp.where(seen, s[i * blk :], -1e30)
         s = jnp.concatenate([s[: i * blk], diag], axis=0) if i else diag
         p = jnp.exp(s - jnp.max(s, axis=0, keepdims=True))
         p = p * (1.0 / jnp.sum(p, axis=0, keepdims=True))
         pb = p.astype(bf16)
-        o = dot(vb[:, :kk], pb)
-        dp = dot(values[:kk], do_t[:, sl])
-        mean = jnp.sum(o * do_t[:, sl].astype(f32), axis=0, keepdims=True)
-        ds = (p * (dp - mean)).astype(bf16)
-        outs.append(o.astype(bf16))
-        dqs.append(dot(kb[:, :kk], ds) * 0.125)
-        dv, dk = dot(pb, grads[sl]), dot(ds, queries[sl])
-        for j in range(i + 1):
-            a, b = dv[j * blk : (j + 1) * blk], dk[j * blk : (j + 1) * blk]
-            dv_sum[j] = a if dv_sum[j] is None else dv_sum[j] + a
-            dk_sum[j] = b if dk_sum[j] is None else dk_sum[j] + b
+        outs.append(dot(vb[:, :kk], pb).astype(bf16))
+        gather(dv_sum, i, dot(pb, grads[sl]))
+        if behind is not None:
+            back(*behind)
+        behind = (i, p, dp)
+    back(*behind)
     dq_t = turn(jnp.concatenate(dqs, axis=1), cos, sin, -1.0)
     dk_t = turn(jnp.concatenate(dk_sum, axis=0).T, cos, sin, -1.0)
     dv_t = jnp.concatenate(dv_sum, axis=0).T
     return jnp.concatenate(outs, axis=1), dq_t, dk_t, dv_t
 
 
+def gelu_and_slope(u):
+    half = 0.5 + 0.5 * lax.erf(u * (1.0 / math.sqrt(2.0)))
+    bell = jnp.exp(u * u * -0.5) * (1.0 / math.sqrt(2.0 * math.pi))
+    return u * half, half + u * bell
+
+
 RW = 256
 RQ = RW // 4
-NS = 6
+NS = 4
+NP = 2
 KINDS = ("P", "A1", "A2", "A3", "A4", "A5", "B1", "B2", "B3", "B4", "B5a", "B5b", "G")
 KI = {k: i for i, k in enumerate(KINDS)}
+HEAD_TICKS = (2, 4, 5, 6, 7, 8, 8, 9)
+LATE = HEAD_TICKS[-1] + 1
+BC = 512
+WC = 256
+N_LOADS = 3
 
 
 def mega_kernel(
-    n_ff, heads,
-    ffg, h, g, w_t, bq, wo, cs, ffb, ffd, resid, vecs, small_in,
+    heads,
+    g_n, r_n, w_qkv, wo, w_up, w_down, bq, bu, cs, ln_gain, ln_bias, b_out, b_down,
     red, out, grad_in, small_out,
-    x_buf, own, ag, fin, ra1, ra2, ra3, rb1, rb2, rb3,
-    qkv_s, do_s, dqkv_t, att_t, dh_own, br_send, br_recv, dh_send, dh_recv, ff_buf, rs_buf, sm_send, sm_recv, sums,
-    ss, rs, own_sem, loc_sem, x_ss, x_rs, ff_sem, sm_ss, sm_rs, fin_sem,
+    act2, dup2, h2, g2, r2, w_t2, wo2, x_buf, fw, ag, fin, ra1, ra2, ra3, rb1, rb2, rb3,
+    qkv_s, do_s, dqkv_t, att_t, t_buf, bq_s, acc, acc2, wd, wu,
+    sm_send, sm_recv, sums,
+    ss, rs, loc_sem, load_sem, r_ss, r_rs, g_ss, g_rs, x_ss, x_rs, wd_sem, wu_sem, sm_ss, sm_rs, out_sem, free_sem,
 ):
+    half, width = g_n.shape
+    hidden = w_down.shape[0]
+    n_g = width // RW
+    n_ff = n_g + n_g
     n_at = heads // 2
     waves = n_ff + n_at
     dp, x = lax.axis_index("dp"), lax.axis_index("tensor")
@@ -106,11 +131,49 @@
     xp = dev(z, y, c, 1 - x)
     inner = jnp.logical_or(z == 1, z == 2)
     outer = jnp.logical_not(inner)
+    near = pl.ds(pl.multiple_of(x * half, half), half)
+    far = pl.ds(pl.multiple_of((1 - x) * half, half), half)
+
+    loads = []
+    for src, dst in ((r_n, r2.at[near]), (g_n, g2.at[near]), (wo, wo2)):
+        loads.append(pltpu.make_async_copy(src, dst, load_sem.at[len(loads)]))
+    for k in loads:
+        k.start()
 
     barrier = pltpu.get_barrier_semaphore()
-    for d in (sib, yp, zp, zm, xp):
+    for d in (xp, sib, yp, zp, zm):
         pl.semaphore_signal(barrier, inc=1, device_id=d, device_id_type=MESH)
     pl.semaphore_wait(barrier, 5)
+
+    def g_copy(i):
+        cols = pl.ds(pl.multiple_of(i * RW, RW), RW)
+        return pltpu.make_async_remote_copy(
+            src_ref=g_n.at[:, cols], dst_ref=g2.at[near, cols], send_sem=g_ss.at[i], recv_sem=g_rs.at[i],
+            device_id=xp, device_id_type=MESH,
+        )
+
+    def g_arrives(i):
+        cols = pl.ds(pl.multiple_of(i * RW, RW), RW)
+        pltpu.make_async_remote_copy(
+            src_ref=g_n.at[:, cols], dst_ref=g2.at[far, cols], send_sem=g_ss.at[i], recv_sem=g_rs.at[i],
+            device_id=xp, device_id_type=MESH,
+        ).wait_recv()
+
+    rb = 256
+    n_rb = half // rb
+
+    def rows_of(who, i):
+        return pl.ds(pl.multiple_of(who * half + i * rb, rb), rb)
+
+    def r_copy(i, who):
+        return pltpu.make_async_remote_copy(
+            src_ref=r_n.at[pl.ds(pl.multiple_of(i * rb, rb), rb)], dst_ref=r2.at[rows_of(who, i)],
+            send_sem=r_ss.at[i], recv_sem=r_rs.at[i], device_id=xp, device_id_type=MESH,
+        )
+
+    for i in range(n_rb):
+        r_copy(i, x).start()
+
 
     a_mine = pl.ds(pl.multiple_of(y * RQ, RQ), RQ)
     a_other = pl.ds(pl.multiple_of((1 - y) * RQ, RQ), RQ)
@@ -154,19 +217,14 @@
             return rc(kind, w, fin.at[w], there, sib)
 
     def p_ff(w):
-        return rc("P", w, ffg.at[w, pl.ds(pl.multiple_of((1 - c) * RW, RW), RW)], x_buf.at[w], sib)
+        return rc("P", w, fw.at[lax.rem(w, 2), 1 - c], x_buf.at[w], sib)
 
     def p_at(j):
-        return rc("P", n_ff + j, ag.at[2 * j + 1 - c], x_buf.at[n_ff + j], sib)
+        return rc("P", n_ff + j, ag.at[lax.rem(j, NP), 1 - c], x_buf.at[n_ff + j], sib)
 
     def local(w):
         here = red.at[w, pl.ds(pl.multiple_of(c * RW, RW), RW)]
         return pltpu.make_async_copy(fin.at[w], here, loc_sem.at[w])
-
-    def own_copy(w):
-        return pltpu.make_async_copy(
-            ffg.at[w, pl.ds(pl.multiple_of(c * RW, RW), RW)], own.at[lax.rem(w, 2)], own_sem.at[lax.rem(w, 2)]
-        )
 
     def add(a, b):
         return (a.astype(f32) + b.astype(f32)).astype(bf16)
@@ -179,18 +237,13 @@
 
             @pl.when(jnp.logical_and(ok, w < n_ff))
             def _():
-                @pl.when(w + 1 < n_ff)
-                def _():
-                    own_copy(w + 1).start()
-
                 p_ff(w).wait_recv()
-                own_copy(w).wait()
-                x_buf[w] = add(x_buf[w], own[lax.rem(w, 2)])
+                x_buf[w] = add(x_buf[w], fw[lax.rem(w, 2), c])
 
             @pl.when(jnp.logical_and(ok, w >= n_ff))
             def _():
                 p_at(w - n_ff).wait_recv()
-                x_buf[w] = add(x_buf[w], ag[2 * (w - n_ff) + c])
+                x_buf[w] = add(x_buf[w], ag[lax.rem(w - n_ff, NP), c])
 
             @pl.when(ok)
             def _():
@@ -268,100 +321,297 @@
                 local(w).start()
 
 
-    cos, sin = cs[0:8], cs[8:16]
-
-    def head(t):
-        qr = pl.ds(pl.multiple_of(t * 192, 64), 192)
-        vr = pl.ds(pl.multiple_of(t * 64, 64), 64)
-        qkv_s[...] = dot_nt(w_t[qr], h[...]) + bq[qr]
-        do_s[...] = dot_nt(wo[vr], g[...]).astype(bf16)
-        o, dq, dk, dv = attend_head(qkv_s[0:64], qkv_s[64:128], qkv_s[128:192], do_s[...], cos, sin)
-        att_t[vr] = o
-        dqkv_t[pl.ds(pl.multiple_of(t * 192, 64), 64)] = dq.astype(bf16)
-        dqkv_t[pl.ds(pl.multiple_of(t * 192 + 64, 64), 64)] = dk.astype(bf16)
-        dqkv_t[pl.ds(pl.multiple_of(t * 192 + 128, 64), 64)] = dv.astype(bf16)
-        ag[t, 0:192] = dot(dqkv_t[qr], h[...]).astype(bf16)
-        ag[t, 192:256] = dot(att_t[vr], g[...]).astype(bf16)
-
-    ch = 128
-    n_ch = out.shape[0] // ch
-
-    def xcopy(which, i):
-        src, dst = ((br_send, br_recv), (dh_send, dh_recv))[which]
-        r = pl.ds(pl.multiple_of(i * ch, ch), ch)
-        return pltpu.make_async_remote_copy(
-            src_ref=src.at[r], dst_ref=dst.at[r], send_sem=x_ss.at[which, i], recv_sem=x_rs.at[which, i],
-            device_id=xp, device_id_type=MESH,
-        )
-
-    def load(src, row, buf, sem):
-        k = pltpu.make_async_copy(src.at[pl.ds(row, ch)], buf, sem)
-        k.start()
-        k.wait()
-
-    def norm(i):
-        r = resid[i].astype(f32)
+    def ff_wave(w):
+        @pl.when(w >= 2)
+        def _():
+            p_ff(w - 2).wait_send()
+
+        def product(src, full):
+            t_buf[...] = src.T
+
+            def block(n, _):
+                cols = pl.ds(pl.multiple_of(n * BC, BC), BC)
+                per = width // BC
+                fw[lax.rem(w, 2), n // per, :, pl.ds(pl.multiple_of(lax.rem(n, per) * BC, BC), BC)] = dot(
+                    t_buf[...], full[:, cols]
+                ).astype(bf16)
+                return 0
+
+            lax.fori_loop(0, hidden // BC, block, 0)
+
+        @pl.when(w < n_g)
+        def _():
+            g_arrives(w)
+            product(g2[:, pl.ds(pl.multiple_of(w * RW, RW), RW)], act2)
+
+        @pl.when(w >= n_g)
+        def _():
+            product(h2[:, pl.ds(pl.multiple_of((w - n_g) * RW, RW), RW)], dup2)
+
+        p_ff(w).start()
+
+    def stream(copy, n, body):
+        copy(0).start()
+
+        def step(i, _):
+            @pl.when(i + 1 < n)
+            def _():
+                copy(i + 1).start()
+
+            copy(i).wait()
+            body(i, lax.rem(i, 2))
+            return 0
+
+        lax.fori_loop(0, n, step, 0)
+
+    def wd_copy(i):
+        s = lax.rem(i, 2)
+        return pltpu.make_async_copy(w_down.at[pl.ds(pl.multiple_of(i * WC, WC), WC)], wd.at[s], wd_sem.at[s])
+
+    def wu_copy(i):
+        s = lax.rem(i, 2)
+        return pltpu.make_async_copy(w_up.at[:, pl.ds(pl.multiple_of(i * WC, WC), WC)], wu.at[s], wu_sem.at[s])
+
+    def wq_copy(i):
+        s = lax.rem(i, 2)
+        return pltpu.make_async_copy(w_qkv.at[:, pl.ds(pl.multiple_of(i * WC, WC), WC)], wu.at[s], wu_sem.at[s])
+
+    class both:
+        def __init__(self, *copies):
+            self.copies = copies
+
+        def start(self):
+            for k in self.copies:
+                k.start()
+
+        def wait(self):
+            for k in self.copies:
+                k.wait()
+
+    n_hid = hidden // WC
+
+    def norm(rows):
+        r = r2[rows].astype(f32)
         centered = r - jnp.mean(r, axis=1, keepdims=True)
         inv = lax.rsqrt(jnp.mean(centered * centered, axis=1, keepdims=True) + epsilon)
         return r, centered * inv, inv
 
-    def rows_of(who, i):
-        return pl.multiple_of(who * (n_ch * ch) + i * ch, ch)
-
-    def branch(row):
-        return dot(att_t[:, pl.ds(row, ch)].T, wo[...])
-
-    def back(row):
-        return dot(dqkv_t[:, pl.ds(row, ch)].T, w_t[...])
-
-    def add_sums(d, row):
-        _, normed, _ = norm(pl.ds(row, ch))
-        sums[0:1] = sums[0:1] + jnp.sum(d * normed, axis=0, keepdims=True)
-        sums[1:2] = sums[1:2] + jnp.sum(d, axis=0, keepdims=True)
-
-    def branch_far(i, _):
-        row = rows_of(1 - x, i)
-        load(ffb, row, ff_buf, ff_sem.at[0])
-        br_send[pl.ds(pl.multiple_of(i * ch, ch), ch)] = (branch(row) + ff_buf[...]).astype(bf16)
-        xcopy(0, i).start()
-        return 0
-
-    def back_far(i, _):
-        row = rows_of(1 - x, i)
-        load(ffd, row, ff_buf, ff_sem.at[0])
-        d = back(row) + ff_buf[...]
-        add_sums(d, row)
-        dh_send[pl.ds(pl.multiple_of(i * ch, ch), ch)] = d.astype(bf16)
-        xcopy(1, i).start()
-        return 0
-
-    def back_near(i, _):
-        row = rows_of(x, i)
-        load(ffd, row, ff_buf, ff_sem.at[0])
-        d = back(row) + ff_buf[...]
-        add_sums(d, row)
-        dh_own[pl.ds(pl.multiple_of(i * ch, ch), ch)] = d
-        return 0
-
-    def branch_near(i, _):
-        row = rows_of(x, i)
-        here = pl.ds(pl.multiple_of(i * ch, ch), ch)
-        load(ffb, row, ff_buf, ff_sem.at[0])
-        xcopy(0, i).wait_recv()
-        total = branch(row) + ff_buf[...] + br_recv[here].astype(f32)
-        out[here] = (resid[pl.ds(row, ch)].astype(f32) + total + vecs[1:2]).astype(bf16)
-        return 0
-
-    def finish(i, _):
-        row = rows_of(x, i)
-        here = pl.ds(pl.multiple_of(i * ch, ch), ch)
-        xcopy(1, i).wait_recv()
-        _, normed, inv = norm(pl.ds(row, ch))
-        d_hat = (dh_own[here] + dh_recv[here].astype(f32)) * vecs[0:1]
-        first = jnp.mean(d_hat, axis=1, keepdims=True)
-        second = jnp.mean(d_hat * normed, axis=1, keepdims=True)
-        grad_in[here] = g[pl.ds(row, ch)].astype(f32) + inv * (d_hat - first - normed * second)
-        return 0
+    def make_hidden(rows):
+        h2[rows] = (norm(rows)[1] * ln_gain[...] + ln_bias[...]).astype(bf16)
+
+    def turn_weights():
+        def body(n, s):
+            w_t2[pl.ds(pl.multiple_of(n * WC, WC), WC)] = wu[s].T
+
+        stream(wq_copy, w_qkv.shape[1] // WC, body)
+        for n in range(w_qkv.shape[1] // 128):
+            cols = slice(n * 128, (n + 1) * 128)
+            bq_s[cols] = jnp.broadcast_to(bq[:, cols], (128, 128)).T
+
+    def ff_near():
+        def body(n, s):
+            cols = pl.ds(pl.multiple_of(n * WC, WC), WC)
+
+            def block(i, _):
+                r = rows_of(x, i)
+                a, slope = gelu_and_slope(dot(h2[r], wu[s]) + bu[:, cols])
+                act2[r, cols] = a.astype(bf16)
+                dup2[r, cols] = (dot_nt(g2[r], wd[s]) * slope).astype(bf16)
+                return 0
+
+            lax.fori_loop(0, n_rb, block, 0)
+
+        stream(lambda i: both(wu_copy(i), wd_copy(i)), n_hid, body)
+
+    def ff_far(i):
+        r = rows_of(1 - x, i)
+        r_copy(i, 1 - x).wait_recv()
+        make_hidden(r)
+
+        def body(n, s):
+            cols = pl.ds(pl.multiple_of(n * WC, WC), WC)
+            a, slope = gelu_and_slope(dot(h2[r], wu[s]) + bu[:, cols])
+            act2[r, cols] = a.astype(bf16)
+            dup2[r, cols] = slope.astype(bf16)
+
+        stream(wu_copy, n_hid, body)
+
+    def d_up_far():
+        def body(n, s):
+            cols = pl.ds(pl.multiple_of(n * WC, WC), WC)
+
+            def block(i, _):
+                r = rows_of(1 - x, i)
+                dup2[r, cols] = (dot_nt(g2[r], wd[s]) * dup2[r, cols].astype(f32)).astype(bf16)
+                return 0
+
+            lax.fori_loop(0, n_rb, block, 0)
+
+        stream(wd_copy, n_hid, body)
+
+
+    cos, sin = cs[0:8], cs[8:16]
+    hq, hv = 3 * HD, HD
+
+    def head(t):
+        odd = lax.rem(t, 2)
+        j = t // 2
+        pair_q = pl.ds(pl.multiple_of(j * 2 * hq, 2 * HD), 2 * hq)
+        pair_v = pl.ds(pl.multiple_of(j * 2 * hv, 2 * HD), 2 * hv)
+
+        @pl.when(odd == 0)
+        def _():
+            qkv_s[...] = dot_nt(w_t2[pair_q], h2[...]) + bq_s[pair_q, 0:1]
+            do_s[...] = dot_nt(wo2[pair_v], g2[...]).astype(bf16)
+
+        part = lambda i: qkv_s[pl.ds(pl.multiple_of(odd * hq + i * HD, HD), HD)]
+        o, dq, dk, dv = attend_head(
+            part(0), part(1), part(2), do_s[pl.ds(pl.multiple_of(odd * hv, HD), HD)], cos, sin
+        )
+        att_t[pl.ds(pl.multiple_of(t * hv, HD), HD)] = o
+        for i, v in enumerate((dq, dk, dv)):
+            dqkv_t[pl.ds(pl.multiple_of(t * hq + i * HD, HD), HD)] = v.astype(bf16)
+
+        @pl.when(odd == 1)
+        def _():
+            slot = lax.rem(j, NP)
+
+            @pl.when(j >= NP)
+            def _():
+                p_at(j - NP).wait_send()
+
+            gq = dot(dqkv_t[pair_q], h2[...]).astype(bf16)
+            gv = dot(att_t[pair_v], g2[...]).astype(bf16)
+            for i in range(2):
+                ag[slot, i, 0:hq] = gq[i * hq : (i + 1) * hq]
+                ag[slot, i, hq : hq + hv] = gv[i * hv : (i + 1) * hv]
+            p_at(j).start()
+
+
+    def xcopy(which, i):
+        dst = h2
+        r = pl.ds(pl.multiple_of(which * half + i * rb, rb), rb)
+        return pltpu.make_async_remote_copy(
+            src_ref=fw.at[which, i], dst_ref=dst.at[r], send_sem=x_ss.at[which, i], recv_sem=x_rs.at[which, i],
+            device_id=xp, device_id_type=MESH,
+        )
+
+    def each(body):
+        def step(i, _):
+            body(i, pl.ds(pl.multiple_of(i * rb, rb), rb))
+            return 0
+
+        lax.fori_loop(0, n_rb, step, 0)
+
+    def branch(who, total):
+        def start(i, here):
+            total[here] = dot(att_t[:, rows_of(who, i)].T, wo2[...])
+
+        each(start)
+
+        def body(n, s):
+            cols = pl.ds(pl.multiple_of(n * WC, WC), WC)
+
+            def block(i, here):
+                total[here] = total[here] + dot(act2[rows_of(who, i), cols], wd[s])
+
+            each(block)
+
+        stream(wd_copy, n_hid, body)
+
+    def back(who, total):
+        def start(i, here):
+            total[here] = dot(dqkv_t[:, rows_of(who, i)].T, w_t2[...])
+
+        each(start)
+
+        def body(n, s):
+            cols = pl.ds(pl.multiple_of(n * WC, WC), WC)
+
+            def block(i, here):
+                total[here] = total[here] + dot_nt(dup2[rows_of(who, i), cols], wu[s])
+
+            each(block)
+
+        stream(wu_copy, n_hid, body)
+
+        def add_sums(i, here):
+            _, normed, _ = norm(rows_of(who, i))
+            d = total[here]
+            sums[0:1] = sums[0:1] + jnp.sum(d * normed, axis=0, keepdims=True)
+            sums[1:2] = sums[1:2] + jnp.sum(d, axis=0, keepdims=True)
+
+        each(add_sums)
+
+    def out_copy():
+        return pltpu.make_async_copy(h2.at[pl.ds(0, half)], out, out_sem.at[0])
+
+    def branch_far():
+        branch(1 - x, acc)
+        pl.semaphore_wait(free_sem, 1)
+
+        def send(i, here):
+            fw[0, i] = acc[here].astype(bf16)
+            xcopy(0, i).start()
+
+        each(send)
+
+    def back_far():
+        back(1 - x, acc)
+
+        def send(i, here):
+            fw[1, i] = acc[here].astype(bf16)
+            xcopy(1, i).start()
+
+        each(send)
+
+    def branch_near():
+        for i in range(n_rb):
+            r = rows_of(x, i)
+            acc2[...] = dot(att_t[:, r].T, wo2[...]) + (b_out[...] + b_down[...])
+
+            def body(n, s):
+                cols = pl.ds(pl.multiple_of(n * WC, WC), WC)
+                acc2[...] = acc2[...] + dot(act2[r, cols], wd[s])
+
+            stream(wd_copy, n_hid, body)
+            xcopy(0, i).wait_recv()
+            here = pl.ds(i * rb, rb)
+            h2[here] = (r2[r].astype(f32) + acc2[...] + h2[here].astype(f32)).astype(bf16)
+        out_copy().start()
+
+    def finish():
+        def last(i, here):
+            xcopy(1, i).wait_recv()
+            _, normed, inv = norm(rows_of(x, i))
+            d_hat = (acc[here] + h2[pl.ds(pl.multiple_of(half + i * rb, rb), rb)].astype(f32)) * ln_gain[...]
+            first = jnp.mean(d_hat, axis=1, keepdims=True)
+            second = jnp.mean(d_hat * normed, axis=1, keepdims=True)
+            acc[here] = g2[rows_of(x, i)].astype(f32) + inv * (d_hat - first - normed * second)
+
+        each(last)
+        pltpu.make_async_copy(acc, grad_in, out_sem.at[1]).start()
+
+    def column_sums(ref, k):
+        parts = []
+        for p in range(2):
+            parts.append(
+                lax.fori_loop(
+                    0, half // 128,
+                    lambda i, t: t + jnp.sum(ref[pl.ds(pl.multiple_of(p * half + i * 128, 128), 128), k].astype(f32), axis=0, keepdims=True),
+                    jnp.zeros((1, width), f32),
+                )
+            )
+        return parts[0] + parts[1]
+
+    def small_fill():
+        n_up = hidden // width
+        for i in range(n_up):
+            sm_send[0, i : i + 1] = column_sums(dup2, slice(i * width, (i + 1) * width))
+        sm_send[0, n_up : n_up + 1] = column_sums(g2, slice(0, width))
+        bias = dot_nt(jnp.ones((8, 2 * half), bf16), dqkv_t[...])
+        sm_send[0, 3:4] = bias[0:1, :width]
+        sm_send[0, 4:5, 0 : bias.shape[1] - width] = bias[0:1, width:]
 
     def small(i):
         device = (sib, yp, zp, zm, xp)[i]
@@ -371,55 +621,67 @@
         )
 
 
-    def start_ff(w, _):
-        p_ff(w).start()
-        return 0
-
-    own_copy(0).start()
-    lax.fori_loop(0, n_ff, start_ff, 0)
     sums[...] = jnp.zeros_like(sums)
+    sm_send[0] = jnp.zeros_like(sums)
+    turn_weights()
+    loads[0].wait()
+    loads[1].wait()
+    for i in range(n_rb):
+        make_hidden(rows_of(x, i))
+    ff_near()
+    for i in range(n_rb):
+        ff_far(i)
+        if i == n_rb - 2:
+            r_copy(n_rb - 1, 1 - x).wait_send()
+            for k in range(n_g):
+                g_copy(k).start()
+    loads[2].wait()
+    ff_wave(0)
 
     def tick(t, _):
-        for s in range(1, 7):
+        for s in range(6, 0, -1):
             stage(s, t)
 
-        @pl.when(t < heads)
-        def _():
-            head(t)
-
-            @pl.when(lax.rem(t, 2) == 1)
-            def _():
-                p_at(t // 2).start()
-
-        at = lambda k: pl.when(t == heads + k)
+        @pl.when(t == n_g - 1)
+        def _():
+            d_up_far()
+
+        @pl.when(t + 1 < n_ff)
+        def _():
+            ff_wave(t + 1)
+
+        done = sum(jnp.where(t > k, 1, 0) for k in HEAD_TICKS)
+        todo = sum(jnp.where(t >= k, 1, 0) for k in HEAD_TICKS)
+
+        def one(i, _):
+            head(i)
+            return 0
+
+        lax.fori_loop(done, todo, one, 0)
+        at = lambda k: pl.when(t == LATE + k)
 
         @at(0)
         def _():
-            lax.fori_loop(0, n_ch, branch_far, 0)
+            pl.semaphore_signal(free_sem, inc=1, device_id=xp, device_id_type=MESH)
+            p_ff(n_ff - 2).wait_send()
+            p_ff(n_ff - 1).wait_send()
+            branch_far()
+            back_far()
 
         @at(1)
         def _():
-            lax.fori_loop(0, n_ch, back_far, 0)
-
-        @at(2)
-        def _():
-            lax.fori_loop(0, n_ch, back_near, 0)
-            ones = jnp.ones((8, dqkv_t.shape[1]), bf16)
-            bias = dot_nt(ones, dqkv_t[...])
-            sm_send[0] = small_in[...]
-            wide = small_in.shape[1]
-            sm_send[0, 3:4] = bias[0:1, :wide]
-            sm_send[0, 4:5, 0 : bias.shape[1] - wide] = bias[0:1, wide:]
+            back(x, acc)
+            small_fill()
             sm_send[0, 5:7] = sums[0:2]
             small(0).start()
 
-        @at(3)
-        def _():
-            lax.fori_loop(0, n_ch, branch_near, 0)
+        @at(2)
+        def _():
+            branch_near()
 
         for k in range(1, 6):
 
-            @at(2 + k)
+            @at(1 + k)
             def _():
                 small(k - 1).wait_recv()
                 total = sm_send[k - 1] + sm_recv[k - 1]
@@ -433,9 +695,9 @@
                 else:
                     small_out[5:7] = total[5:7]
 
-        @at(8)
-        def _():
-            lax.fori_loop(0, n_ch, finish, 0)
+        @at(5)
+        def _():
+            finish()
 
         return 0
 
@@ -457,42 +719,41 @@
             for k in ("B2", "A3", "B3", "A4", "B4", "B5a", "B5b"):
                 cp(k, w).wait_send()
 
-        @pl.when(w < n_ff)
-        def _():
-            p_ff(w).wait_send()
-
-        @pl.when(w >= n_ff)
-        def _():
-            p_at(w - n_ff).wait_send()
-
         return 0
 
     lax.fori_loop(0, waves, drain, 0)
-
-    def drain_x(i, _):
+    for i in range(NP):
+        p_at(n_at - NP + i).wait_send()
+    for i in range(n_rb):
         xcopy(0, i).wait_send()
         xcopy(1, i).wait_send()
-        return 0
-
-    lax.fori_loop(0, n_ch, drain_x, 0)
+    for i in range(n_rb - 1):
+        r_copy(i, x).wait_send()
+    for i in range(n_g):
+        g_copy(i).wait_send()
     for i in range(5):
         small(i).wait_send()
-
-
-def mega(ffg, h, g, w_t, bq, wo, cs, ffb, ffd, resid, vecs, small_in):
-    rows, width = h.shape
+    out_copy().wait()
+    pltpu.make_async_copy(acc, grad_in, out_sem.at[1]).wait()
+
+
+def mega(g_n, r_n, w_qkv, wo, w_up, w_down, *small):
+    half, width = g_n.shape
+    rows = 2 * half
+    hidden = w_down.shape[0]
     heads = wo.shape[0] // HD
-    n_ff = ffg.shape[0]
-    waves = n_ff + heads // 2
-    half = rows // 2
-    n_ch = half // 128
+    n_g = width // RW
+    waves = 2 * n_g + heads // 2
+    n_rb = half // 256
     vm = pl.BlockSpec(memory_space=pltpu.VMEM)
     hbm = pl.BlockSpec(memory_space=pl.ANY)
     dma = pltpu.SemaphoreType.DMA
+    v16 = lambda *s: pltpu.VMEM(s, bf16)
+    v32 = lambda *s: pltpu.VMEM(s, f32)
     return pl.pallas_call(
-        functools.partial(mega_kernel, n_ff, heads),
-        in_specs=[hbm, vm, vm, vm, vm, vm, vm, hbm, hbm, vm, vm, vm],
-        out_specs=[hbm, vm, vm, vm],
+        functools.partial(mega_kernel, heads),
+        in_specs=[hbm] * 6 + [vm] * len(small),
+        out_specs=[hbm, hbm, hbm, vm],
         out_shape=[
             jax.ShapeDtypeStruct((waves, 2 * RW, width), bf16),
             jax.ShapeDtypeStruct((half, width), bf16),
@@ -500,96 +761,86 @@
             jax.ShapeDtypeStruct((8, width), f32),
         ],
         scratch_shapes=[
-            pltpu.VMEM((waves, RW, width), bf16),
-            pltpu.VMEM((2, RW, width), bf16),
-            pltpu.VMEM((heads, RW, width), bf16),
-            pltpu.VMEM((waves, RW, width), bf16),
-            pltpu.VMEM((NS, RQ, width), bf16),
-            pltpu.VMEM((NS, RQ, width), bf16),
-            pltpu.VMEM((NS, RQ, width), bf16),
-            pltpu.VMEM((NS, 2 * RQ, width), bf16),
-            pltpu.VMEM((NS, RQ, width), bf16),
-            pltpu.VMEM((NS, RQ, width), bf16),
-            pltpu.VMEM((3 * HD, rows), f32),
-            pltpu.VMEM((HD, rows), bf16),
-            pltpu.VMEM((heads * 3 * HD, rows), bf16),
-            pltpu.VMEM((heads * HD, rows), bf16),
-            pltpu.VMEM((half, width), f32),
-            pltpu.VMEM((half, width), bf16),
-            pltpu.VMEM((half, width), bf16),
-            pltpu.VMEM((half, width), bf16),
-            pltpu.VMEM((half, width), bf16),
-            pltpu.VMEM((128, width), f32),
-            pltpu.VMEM((8, width), f32),
-            pltpu.VMEM((5, 8, width), f32),
-            pltpu.VMEM((5, 8, width), f32),
-            pltpu.VMEM((8, width), f32),
-            dma((len(KINDS), waves)),
-            dma((len(KINDS), waves)),
-            dma((2,)),
-            dma((waves,)),
-            dma((2, n_ch)),
-            dma((2, n_ch)),
-            dma((2,)),
-            dma((5,)),
-            dma((5,)),
-            dma((2,)),
+            v16(rows, hidden), v16(rows, hidden), v16(rows, width), v16(rows, width), v16(rows, width),
+            v16(heads * 3 * HD, width), v16(heads * HD, width),
+            v16(waves, RW, width), v16(2, 2, RW, width), v16(NP, 2, RW, width), v16(waves, RW, width),
+            v16(NS, RQ, width), v16(NS, RQ, width), v16(NS, RQ, width), v16(NS, 2 * RQ, width), v16(NS, RQ, width), v16(NS, RQ, width),
+            v32(6 * HD, rows), v16(2 * HD, rows), v16(heads * 3 * HD, rows), v16(heads * HD, rows), v16(RW, rows),
+            v32(heads * 3 * HD, 128), v32(half, width), v32(256, width),
+            v16(2, WC, width), v16(2, width, WC),
+            v32(5, 8, width), v32(5, 8, width), v32(8, width),
+            dma((len(KINDS), waves)), dma((len(KINDS), waves)), dma((waves,)), dma((N_LOADS,)), dma((n_rb,)), dma((n_rb,)),
+            dma((n_g,)), dma((n_g,)), dma((2, n_rb)), dma((2, n_rb)), dma((2,)), dma((2,)), dma((5,)), dma((5,)), dma((2,)), pltpu.SemaphoreType.REGULAR,
         ],
-        compiler_params=pltpu.CompilerParams(collective_id=0, has_side_effects=True, vmem_limit_bytes=62 * 2**20),
+        compiler_params=pltpu.CompilerParams(collective_id=0, has_side_effects=True, vmem_limit_bytes=63 * 2**20),
         name="attention_and_sums",
-    )(ffg, h, g, w_t, bq, wo, cs, ffb, ffd, resid, vecs, small_in)
+    )(g_n, r_n, w_qkv, wo, w_up, w_down, *small)
+
+
+def widen_kernel(n_g, src, down, up, qkv, out):
+    i = pl.program_id(0)
+    width = src.shape[2]
+    side = lambda k: lax.broadcasted_iota(jnp.int32, (RW, RW), k)
+    eye = jnp.where(side(0) == side(1), 1.0, 0.0).astype(bf16)
+
+    @pl.when(i < n_g)
+    def _():
+        for c in range(2):
+            for k in range(width // RW):
+                down[c * width + k * RW : c * width + (k + 1) * RW] = dot_nt(
+                    eye, src[0, c * RW : (c + 1) * RW, k * RW : (k + 1) * RW]
+                )
+
+    @pl.when(jnp.logical_and(i >= n_g, i < 2 * n_g))
+    def _():
+        for c in range(2):
+            up[:, c * width : (c + 1) * width] = src[0, c * RW : (c + 1) * RW].astype(f32)
+
+    @pl.when(i >= 2 * n_g)
+    def _():
+        hq = 3 * HD
+        for k in range(width // RW):
+            cols = slice(k * RW, (k + 1) * RW)
+            both = jnp.concatenate([src[0, 0:hq, cols], src[0, RW : RW + hq, cols]], axis=0)
+            qkv[cols] = dot_nt(eye, both)
+        for c in range(2):
+            out[c * HD : (c + 1) * HD] = src[0, c * RW + hq : (c + 1) * RW].astype(f32)
+
+
+def widen(red, hidden):
+    waves, _, width = red.shape
+    n_g = width // RW
+    n_at = waves - 2 * n_g
+    clip = lambda i, first, n: jnp.minimum(jnp.maximum(i - first, 0), n - 1)
+    return pl.pallas_call(
+        functools.partial(widen_kernel, n_g),
+        grid=(waves,),
+        in_specs=[pl.BlockSpec((1, 2 * RW, width), lambda i: (i, 0, 0))],
+        out_specs=[
+            pl.BlockSpec((hidden, RW), lambda i: (0, clip(i, 0, n_g))),
+            pl.BlockSpec((RW, hidden), lambda i: (clip(i, n_g, n_g), 0)),
+            pl.BlockSpec((width, 6 * HD), lambda i: (0, clip(i, 2 * n_g, n_at))),
+            pl.BlockSpec((2 * HD, width), lambda i: (clip(i, 2 * n_g, n_at), 0)),
+        ],
+        out_shape=[
+            jax.ShapeDtypeStruct((hidden, width), f32),
+            jax.ShapeDtypeStruct((width, hidden), f32),
+            jax.ShapeDtypeStruct((width, n_at * 6 * HD), f32),
+            jax.ShapeDtypeStruct((n_at * 2 * HD, width), f32),
+        ],
+        compiler_params=pltpu.CompilerParams(vmem_limit_bytes=48 * 2**20),
+        name="widen",
+    )(red)
 
 
 def shards(residual, ln_gain, ln_bias, w_qkv, b_qkv, w_out, b_out, w_up, b_up, w_down, b_down, grad_out):
-    x = lax.axis_index("tensor")
-    swap = [(0, 1), (1, 0)]
-    far_resid = lax.ppermute(residual, "tensor", swap)
-    grad_first, far_resid = lax.optimization_barrier((grad_out, far_resid))
-    far_grad = lax.ppermute(grad_first, "tensor", swap)
-
-    def group(near, far):
-        return jnp.where(x == 0, jnp.concatenate([near, far]), jnp.concatenate([far, near]))
-
-    resid = group(residual, far_resid)
-    wide = resid.astype(f32)
-    centered = wide - jnp.mean(wide, axis=1, keepdims=True)
-    variance = jnp.mean(centered * centered, axis=1, keepdims=True)
-    normed = centered * lax.rsqrt(variance + epsilon)
-    h = (normed * ln_gain + ln_bias).astype(bf16)
-    g = group(grad_out, far_grad)
-    up_lin = dot(h, w_up) + b_up
-    act_wide, gelu_back = jax.vjp(functools.partial(jax.nn.gelu, approximate=False), up_lin)
-    slope = gelu_back(jnp.ones_like(up_lin))[0].astype(bf16)
-    act = act_wide.astype(bf16)
-    act, slope = lax.optimization_barrier((act, slope))
-    ffb = dot(act, w_down)
-    d_up = (dot_nt(g, w_down) * slope.astype(f32)).astype(bf16)
-    ffd = dot_nt(d_up, w_up)
-    g_down = dot_tn(act, g).astype(bf16)
-    g_up = dot_tn(h, d_up).astype(bf16)
-    rows, width = h.shape
-    n_up = g_up.shape[1] // width
-    blocks = [g_down.reshape(-1, 2 * RW, width)]
-    blocks += [g_up[:, i * width : (i + 1) * width].reshape(-1, 2 * RW, width) for i in range(n_up)]
-    ffg = jnp.concatenate(blocks)
-    n_down = blocks[0].shape[0]
-    gb_up = jnp.sum(d_up, axis=0, dtype=f32)
-    gb_near = jnp.sum(grad_out, axis=0, dtype=f32)
-    gb_far = jnp.sum(far_grad, axis=0, dtype=f32)
-    gb_out = gb_near + gb_far
-    small_in = jnp.concatenate([gb_up.reshape(n_up, width), gb_out[None], jnp.zeros((7 - n_up, width), f32)])
-    cosine, sine = turn_tables(rows)
+    width = residual.shape[1]
+    cosine, sine = turn_tables(2 * residual.shape[0])
     cs = jnp.concatenate([cosine.T, sine.T])
-    vecs = jnp.concatenate([ln_gain[None], (b_out + b_down)[None], jnp.zeros((6, width), f32)])
-    red, out, grad_in, small = mega(ffg, h, g, w_qkv.T, b_qkv[:, None], w_out, cs, ffb, ffd, resid, vecs, small_in)
-    grad_w_down = red[:n_down].reshape(-1, width).astype(f32)
-    per = width // (2 * RW)
-    ups = [red[n_down + i * per : n_down + (i + 1) * per].reshape(width, width) for i in range(n_up)]
-    grad_w_up = jnp.concatenate(ups, axis=1).astype(f32)
-    at = red[n_down + n_up * per :].reshape(-1, RW, width)
-    grad_w_qkv = at[:, : 3 * HD].reshape(-1, width).T.astype(f32)
-    grad_w_out = at[:, 3 * HD :].reshape(-1, width).astype(f32)
-    gb_up = small[:n_up].reshape(-1)
+    rows = [v[None] for v in (b_qkv, b_up)] + [cs] + [v[None] for v in (ln_gain, ln_bias, b_out, b_down)]
+    red, out, grad_in, small = mega(grad_out, residual, w_qkv, w_out, w_up, w_down, *rows)
+    grad_w_down, grad_w_up, grad_w_qkv, grad_w_out = widen(red, w_down.shape[0])
+    gb_up = small[: b_up.shape[0] // width].reshape(-1)
     gb_out = small[2]
     gb_qkv = small[3:5].reshape(-1)[: b_qkv.shape[0]]
     return out, grad_in, small[5], small[6], grad_w_qkv, gb_qkv, grad_w_out, gb_out, grad_w_up, gb_up, grad_w_down, gb_out

time: 302 us -> 228 us (0.75)
  Pallas kernels: 152 us -> 218 us
  matrix products: 58.7 us -> 0 us
  other arithmetic: 39.1 us -> 0.85 us
  local copies, waits for them, and re-layouts: 31.9 us -> 7.11 us
  waiting for transfers between devices: 13.7 us -> 0 us
  starting transfers between devices: 4.81 us -> 0 us
    pallas_call x1 -> x2, Pallas kernels: 152 us -> 218 us  [the longest x1 200 us: mega(): pl.pallas_call(functools.partial(mega_kernel, heads), in_specs=[hbm] * 6...]
    dot_general x6 -> x0, matrix products: 58.7 us -> none  [the longest x2 32.7 us: dot(): lax.dot_general(left, right, (((1,), (0,)), ((), ())), preferred_element_...]
    convert_element_type x6 -> x0, other arithmetic: 25.3 us -> none  [the longest x1 7.98 us: shards(): act = act_wide.astype(bf16)]
    ppermute x2 -> x0, waiting for transfers between devices: 13.7 us -> none  [the longest x1 13.7 us: shards(): far_resid = lax.ppermute(residual, 'tensor', swap)]
    slice x5 -> x0, local copies, waits for them, and re-layouts: 12.7 us -> none  [the longest x1 5.25 us: shards(): grad_w_down = red[:n_down].reshape(-1, width).astype(f32)]
    unnamed x40 -> x10, local copies, waits for them, and re-layouts: 15 us -> 3.73 us
    concatenate x3 -> x0, other arithmetic: 5.16 us -> none  [the longest x1 3.8 us: shards(): ffg = jnp.concatenate(blocks)]
    ppermute x2 -> x0, starting transfers between devices: 4.81 us -> none  [the longest x1 3 us: shards(): far_resid = lax.ppermute(residual, 'tensor', swap)]
  transfers between devices with their start and end apart: 2 -> 0, of which waited for: 1 -> 0; matrix products, arithmetic and copies ran while one was open for 17% -> 0% of each run, Pallas kernels for 0% -> 0%
where the time goes in v2:
time: 228 us; the launch traced here: 226 us
  Pallas kernels  218 us (96%)
  local copies, waits for them, and re-layouts  7.11 us (3%)
    pallas_call x1, Pallas kernels, mega(): pl.pallas_call(functools.partial(mega_kernel, heads), in_specs=[hbm] * 6...  200 us
    pallas_call x1, Pallas kernels, widen(): pl.pallas_call(functools.partial(widen_kernel, n_g), grid=(waves,), in_sp...  17.8 us

profile of v2, /device:TPU:0, one launch (start us, length us, event | category | flops | bytes accessed | tf_op | source)
XLA Modules:
  0.0 226.2 jit_solution(6078720705312022725)
XLA Ops:
  0.7 1.3 broadcast_in_dim.20.bq
  2.0 0.2 fusion.1
  2.2 0.6 pad_maximum_fusion.cs
  2.8 199.8 %attention_and_sums.1 = (bf16[12,512,1024]{2,1,0:T(8,128)(2,1)}, bf16[512,1024]{1,0:T(8,128)(2,1)}, f32[512,1024]{1,0:T(8,128)}, f32[8,1024]{1,0:T(8,128)}) custom-call(bf16[512,1024]{1,0:T(8,128)(2,1)} %g_n.1, bf16[512,1024]{1,0:T(8,128)(2,1)} %r_n.1, bf16[1024,1536]{1,0:T(8,128)(2,1)} %w_qkv.1, bf16[512,1024]{1,0:T(8,128)(2,1)} %wo.1, ...), custom_call_target="tpu_custom_call" | custom-call | tf_op jit(solution)/shard_map/attention_and_sums/pallas_call | solution.py:753
  202.6 1.5 fusion.2
  204.0 0.0 copy-start.2
  204.0 0.8 slice_bitcast_fusion
  204.9 0.6 copy_bitcast_fusion
  205.5 0.0 copy-start.1
  205.5 0.0 copy-start
  205.5 17.8 %widen.1 = (f32[2048,1024]{1,0:T(8,128)}, f32[1024,2048]{1,0:T(8,128)}, f32[1024,1536]{1,0:T(8,128)}, f32[512,1024]{1,0:T(8,128)}) custom-call(bf16[12,512,1024]{2,1,0:T(8,128)(2,1)} %get-tuple-element.23.src), custom_call_target="tpu_custom_call" | custom-call | tf_op jit(solution)/shard_map/widen/pallas_call | solution.py:815
  223.3 0.0 copy-done.2
  223.3 0.6 copy.31
  223.9 0.0 copy-done.1
  223.9 1.0 copy.32
  224.8 0.0 copy-done
  224.8 1.3 copy.33
  (1 shorter events, 0.0 us)
Async XLA Ops:
  204.0 19.2 %copy-start.2 = (f32[1,1024]{1,0:T(1,128)}, f32[1,1024]{1,0:T(1,128)S(1)}, u32[]{:S(2)}) copy-start(f32[1,1024]{1,0:T(1,128)S(1)} %get-tuple-element.30) | copy-start | bytes 12292
  205.5 18.4 %copy-start.1 = (bf16[512,1024]{1,0:T(8,128)(2,1)S(1)}, bf16[512,1024]{1,0:T(8,128)(2,1)}, u32[]{:S(2)}) copy-start(bf16[512,1024]{1,0:T(8,128)(2,1)} %get-tuple-element.73) | copy-start | bytes 3145732
  205.5 19.4 %copy-start = (f32[512,1024]{1,0:T(8,128)S(1)}, f32[512,1024]{1,0:T(8,128)}, u32[]{:S(2)}) copy-start(f32[512,1024]{1,0:T(8,128)} %get-tuple-element.74) | copy-start | bytes 6291460

commit v3 on v2

--- a/solution.py
+++ b/solution.py
@@ -3,6 +3,7 @@
 
 import jax
 import jax.numpy as jnp
+import numpy as np
 from jax import lax
 from jax.experimental import pallas as pl
 from jax.experimental.pallas import tpu as pltpu
@@ -99,28 +100,35 @@
 NP = 2
 KINDS = ("P", "A1", "A2", "A3", "A4", "A5", "B1", "B2", "B3", "B4", "B5a", "B5b", "G")
 KI = {k: i for i, k in enumerate(KINDS)}
-HEAD_TICKS = (2, 4, 5, 6, 7, 8, 8, 9)
-LATE = HEAD_TICKS[-1] + 1
+TURNS = ((6, 5, 4), (3, 2, 1), ())
+FF_AT = (1, 4, 7, 22, 24, 27, 30)
+HEAD_AT = (8, 9, 10, 12, 13, 15, 16, 18)
+PLAN = {
+    "branch_ff": 0, "free": 12, "d_up": 19, "branch_far": 21, "back_far": 25, "back_near": 28, "small": 31,
+    "branch_near": 36, "finish": 45,
+}
+SMALL_AT = (34, 37, 40, 43, 46)
 BC = 512
 WC = 256
-N_LOADS = 3
+N_LOADS = 6
 
 
 def mega_kernel(
     heads,
     g_n, r_n, w_qkv, wo, w_up, w_down, bq, bu, cs, ln_gain, ln_bias, b_out, b_down,
     red, out, grad_in, small_out,
-    act2, dup2, h2, g2, r2, w_t2, wo2, x_buf, fw, ag, fin, ra1, ra2, ra3, rb1, rb2, rb3,
-    qkv_s, do_s, dqkv_t, att_t, t_buf, bq_s, acc, acc2, wd, wu,
+    act2, dup2, h2, g2, r2, w_t2, wo2, w_up2, w_dn2, x_buf, fw, ag, ra1, ra2, ra3, rb1, rb2, rb3,
+    qkv_s, do_s, dqkv_t, att_t, t_buf, tq, acc,
     sm_send, sm_recv, sums,
-    ss, rs, loc_sem, load_sem, r_ss, r_rs, g_ss, g_rs, x_ss, x_rs, wd_sem, wu_sem, sm_ss, sm_rs, out_sem, free_sem,
+    ss, rs, loc_sem, load_sem, r_ss, r_rs, g_ss, g_rs, x_ss, x_rs, sm_ss, sm_rs, out_sem, free_sem, y_free, z_free, m_free,
 ):
     half, width = g_n.shape
     hidden = w_down.shape[0]
     n_g = width // RW
-    n_ff = n_g + n_g
     n_at = heads // 2
+    n_ff = 2 * n_g
     waves = n_ff + n_at
+    first_up = n_g + n_at
     dp, x = lax.axis_index("dp"), lax.axis_index("tensor")
     c, y, z = lax.rem(dp, 2), lax.rem(dp // 2, 2), dp // 4
     dev = lambda zz, yy, cc, xx: (zz * 4 + yy * 2 + cc, xx)
@@ -135,7 +143,10 @@
     far = pl.ds(pl.multiple_of((1 - x) * half, half), half)
 
     loads = []
-    for src, dst in ((r_n, r2.at[near]), (g_n, g2.at[near]), (wo, wo2)):
+    staged = act2.at[:, pl.ds(0, w_qkv.shape[1])]
+    for src, dst in (
+        (w_qkv, staged), (r_n, r2.at[near]), (w_up, w_up2), (g_n, g2.at[near]), (w_down, w_dn2), (wo, wo2),
+    ):
         loads.append(pltpu.make_async_copy(src, dst, load_sem.at[len(loads)]))
     for k in loads:
         k.start()
@@ -197,9 +208,9 @@
         if kind == "A3":
             return rc(kind, w, x_buf.at[w, a_mine], ra3.at[s], zm)
         if kind == "A4":
-            return rc(kind, w, fin.at[w, a_mine], fin.at[w, a_mine], zp)
+            return rc(kind, w, x_buf.at[w, a_mine], x_buf.at[w, a_mine], zp)
         if kind == "A5":
-            return rc(kind, w, fin.at[w, a_mine], fin.at[w, a_mine], yp)
+            return rc(kind, w, x_buf.at[w, a_mine], x_buf.at[w, a_mine], yp)
         if kind == "B1":
             return rc(kind, w, x_buf.at[w, b_all], rb1.at[s], zp)
         if kind == "B2":
@@ -207,27 +218,33 @@
         if kind == "B3":
             return rc(kind, w, x_buf.at[w, b_mine], rb3.at[s], yp)
         if kind == "B4":
-            return rc(kind, w, fin.at[w, b_mine], fin.at[w, b_mine], zm)
+            return rc(kind, w, x_buf.at[w, b_mine], x_buf.at[w, b_mine], zm)
         if kind == "B5a":
-            return rc(kind, w, fin.at[w, b_mine], fin.at[w, b_mine], zp)
+            return rc(kind, w, x_buf.at[w, b_mine], x_buf.at[w, b_mine], zp)
         if kind == "B5b":
-            return rc(kind, w, fin.at[w, b_other], fin.at[w, b_other], zp)
+            return rc(kind, w, x_buf.at[w, b_other], x_buf.at[w, b_other], zp)
         if kind == "G":
             there = red.at[w, pl.ds(pl.multiple_of(c * RW, RW), RW)]
-            return rc(kind, w, fin.at[w], there, sib)
-
-    def p_ff(w):
-        return rc("P", w, fw.at[lax.rem(w, 2), 1 - c], x_buf.at[w], sib)
+            return rc(kind, w, x_buf.at[w], there, sib)
+
+    def wave_of(k):
+        return jnp.where(k < n_g, k, k + n_at)
+
+    def p_ff(k):
+        return rc("P", wave_of(k), fw.at[lax.rem(k, 2), 1 - c], x_buf.at[wave_of(k)], sib)
 
     def p_at(j):
-        return rc("P", n_ff + j, ag.at[lax.rem(j, NP), 1 - c], x_buf.at[n_ff + j], sib)
+        return rc("P", n_g + j, ag.at[lax.rem(j, NP), 1 - c], x_buf.at[n_g + j], sib)
 
     def local(w):
         here = red.at[w, pl.ds(pl.multiple_of(c * RW, RW), RW)]
-        return pltpu.make_async_copy(fin.at[w], here, loc_sem.at[w])
+        return pltpu.make_async_copy(x_buf.at[w], here, loc_sem.at[w])
 
     def add(a, b):
         return (a.astype(f32) + b.astype(f32)).astype(bf16)
+
+    def give(sem, device):
+        pl.semaphore_signal(sem, inc=1, device_id=device, device_id_type=MESH)
 
     def stage(s, t):
         w = t - (s - 1)
@@ -235,15 +252,18 @@
         slot = lax.rem(w, NS)
         if s == 1:
 
-            @pl.when(jnp.logical_and(ok, w < n_ff))
-            def _():
-                p_ff(w).wait_recv()
-                x_buf[w] = add(x_buf[w], fw[lax.rem(w, 2), c])
-
-            @pl.when(jnp.logical_and(ok, w >= n_ff))
-            def _():
-                p_at(w - n_ff).wait_recv()
-                x_buf[w] = add(x_buf[w], ag[lax.rem(w - n_ff, NP), c])
+            of_heads = jnp.logical_and(w >= n_g, w < first_up)
+
+            @pl.when(jnp.logical_and(ok, jnp.logical_not(of_heads)))
+            def _():
+                k = jnp.where(w < n_g, w, w - n_at)
+                p_ff(k).wait_recv()
+                x_buf[w] = add(x_buf[w], fw[lax.rem(k, 2), c])
+
+            @pl.when(jnp.logical_and(ok, of_heads))
+            def _():
+                p_at(w - n_g).wait_recv()
+                x_buf[w] = add(x_buf[w], ag[lax.rem(w - n_g, NP), c])
 
             @pl.when(ok)
             def _():
@@ -257,7 +277,8 @@
 
             @pl.when(ok)
             def _():
-                cp("A1", w).wait_recv()
+                cp("A1", w).wait()
+                give(y_free, yp)
                 x_buf[w, a_mine] = add(x_buf[w, a_mine], ra1[slot])
 
                 @pl.when(outer)
@@ -272,12 +293,19 @@
 
         if s == 3:
 
+            @pl.when(jnp.logical_and(ok, outer))
+            def _():
+                cp("B1", w).wait_send()
+                cp("A2", w).wait_send()
+                give(z_free, zp)
+
             @pl.when(jnp.logical_and(ok, inner))
             def _():
                 cp("A2", w).wait_recv()
                 x_buf[w, a_mine] = add(x_buf[w, a_mine], ra2[slot])
                 cp("A3", w).start()
-                cp("B2", w).wait_recv()
+                cp("B2", w).wait()
+                give(m_free, zm)
                 x_buf[w, b_mine] = add(x_buf[w, b_mine], rb2[slot])
                 cp("B3", w).start()
 
@@ -285,12 +313,15 @@
 
             @pl.when(jnp.logical_and(ok, inner))
             def _():
-                cp("A3", w).wait_recv()
-                fin[w, a_mine] = add(x_buf[w, a_mine], ra3[slot])
+                cp("A3", w).wait()
+                x_buf[w, a_mine] = add(x_buf[w, a_mine], ra3[slot])
+                pl.semaphore_wait(z_free, 1)
                 cp("A4", w).start()
+                pl.semaphore_wait(y_free, 1)
                 cp("A5", w).start()
-                cp("B3", w).wait_recv()
-                fin[w, b_mine] = add(x_buf[w, b_mine], rb3[slot])
+                cp("B3", w).wait()
+                x_buf[w, b_mine] = add(x_buf[w, b_mine], rb3[slot])
+                pl.semaphore_wait(m_free, 1)
                 cp("B4", w).start()
                 cp("B5a", w).start()
 
@@ -304,6 +335,7 @@
             @pl.when(jnp.logical_and(ok, outer))
             def _():
                 cp("A4", w).wait_recv()
+                pl.semaphore_wait(y_free, 1)
                 cp("A5", w).start()
 
         if s == 6:
@@ -321,10 +353,10 @@
                 local(w).start()
 
 
-    def ff_wave(w):
-        @pl.when(w >= 2)
-        def _():
-            p_ff(w - 2).wait_send()
+    def ff_wave(k):
+        @pl.when(k >= 2)
+        def _():
+            p_ff(k - 2).wait_send()
 
         def product(src, full):
             t_buf[...] = src.T
@@ -332,61 +364,23 @@
             def block(n, _):
                 cols = pl.ds(pl.multiple_of(n * BC, BC), BC)
                 per = width // BC
-                fw[lax.rem(w, 2), n // per, :, pl.ds(pl.multiple_of(lax.rem(n, per) * BC, BC), BC)] = dot(
+                fw[lax.rem(k, 2), n // per, :, pl.ds(pl.multiple_of(lax.rem(n, per) * BC, BC), BC)] = dot(
                     t_buf[...], full[:, cols]
                 ).astype(bf16)
                 return 0
 
             lax.fori_loop(0, hidden // BC, block, 0)
 
-        @pl.when(w < n_g)
-        def _():
-            g_arrives(w)
-            product(g2[:, pl.ds(pl.multiple_of(w * RW, RW), RW)], act2)
-
-        @pl.when(w >= n_g)
-        def _():
-            product(h2[:, pl.ds(pl.multiple_of((w - n_g) * RW, RW), RW)], dup2)
-
-        p_ff(w).start()
-
-    def stream(copy, n, body):
-        copy(0).start()
-
-        def step(i, _):
-            @pl.when(i + 1 < n)
-            def _():
-                copy(i + 1).start()
-
-            copy(i).wait()
-            body(i, lax.rem(i, 2))
-            return 0
-
-        lax.fori_loop(0, n, step, 0)
-
-    def wd_copy(i):
-        s = lax.rem(i, 2)
-        return pltpu.make_async_copy(w_down.at[pl.ds(pl.multiple_of(i * WC, WC), WC)], wd.at[s], wd_sem.at[s])
-
-    def wu_copy(i):
-        s = lax.rem(i, 2)
-        return pltpu.make_async_copy(w_up.at[:, pl.ds(pl.multiple_of(i * WC, WC), WC)], wu.at[s], wu_sem.at[s])
-
-    def wq_copy(i):
-        s = lax.rem(i, 2)
-        return pltpu.make_async_copy(w_qkv.at[:, pl.ds(pl.multiple_of(i * WC, WC), WC)], wu.at[s], wu_sem.at[s])
-
-    class both:
-        def __init__(self, *copies):
-            self.copies = copies
-
-        def start(self):
-            for k in self.copies:
-                k.start()
-
-        def wait(self):
-            for k in self.copies:
-                k.wait()
+        @pl.when(k < n_g)
+        def _():
+            g_arrives(k)
+            product(g2[:, pl.ds(pl.multiple_of(k * RW, RW), RW)], act2)
+
+        @pl.when(k >= n_g)
+        def _():
+            product(h2[:, pl.ds(pl.multiple_of((k - n_g) * RW, RW), RW)], dup2)
+
+        p_ff(k).start()
 
     n_hid = hidden // WC
 
@@ -397,57 +391,48 @@
         return r, centered * inv, inv
 
     def make_hidden(rows):
-        h2[rows] = (norm(rows)[1] * ln_gain[...] + ln_bias[...]).astype(bf16)
+        h2[rows] = (norm(rows)[1] * ln_gain[...][None] + ln_bias[...][None]).astype(bf16)
 
     def turn_weights():
-        def body(n, s):
-            w_t2[pl.ds(pl.multiple_of(n * WC, WC), WC)] = wu[s].T
-
-        stream(wq_copy, w_qkv.shape[1] // WC, body)
-        for n in range(w_qkv.shape[1] // 128):
-            cols = slice(n * 128, (n + 1) * 128)
-            bq_s[cols] = jnp.broadcast_to(bq[:, cols], (128, 128)).T
+        def body(n, _):
+            here = pl.ds(pl.multiple_of(n * WC, WC), WC)
+            w_t2[here] = act2[:, here].T
+            return 0
+
+        lax.fori_loop(0, w_qkv.shape[1] // WC, body, 0)
+
+    def over(total, size, body):
+        def step(n, _):
+            body(pl.ds(pl.multiple_of(n * size, size), size))
+            return 0
+
+        lax.fori_loop(0, total // size, step, 0)
 
     def ff_near():
-        def body(n, s):
-            cols = pl.ds(pl.multiple_of(n * WC, WC), WC)
-
-            def block(i, _):
-                r = rows_of(x, i)
-                a, slope = gelu_and_slope(dot(h2[r], wu[s]) + bu[:, cols])
-                act2[r, cols] = a.astype(bf16)
-                dup2[r, cols] = (dot_nt(g2[r], wd[s]) * slope).astype(bf16)
-                return 0
-
-            lax.fori_loop(0, n_rb, block, 0)
-
-        stream(lambda i: both(wu_copy(i), wd_copy(i)), n_hid, body)
+        def body(cols):
+            a, slope = gelu_and_slope(dot(h2[near], w_up2[:, cols]) + bu[cols][None])
+            act2[near, cols] = a.astype(bf16)
+            dup2[near, cols] = (dot_nt(g2[near], w_dn2[cols]) * slope).astype(bf16)
+
+        over(hidden, WC, body)
 
     def ff_far(i):
         r = rows_of(1 - x, i)
         r_copy(i, 1 - x).wait_recv()
         make_hidden(r)
 
-        def body(n, s):
-            cols = pl.ds(pl.multiple_of(n * WC, WC), WC)
-            a, slope = gelu_and_slope(dot(h2[r], wu[s]) + bu[:, cols])
+        def body(cols):
+            a, slope = gelu_and_slope(dot(h2[r], w_up2[:, cols]) + bu[cols][None])
             act2[r, cols] = a.astype(bf16)
             dup2[r, cols] = slope.astype(bf16)
 
-        stream(wu_copy, n_hid, body)
+        over(hidden, BC, body)
 
     def d_up_far():
-        def body(n, s):
-            cols = pl.ds(pl.multiple_of(n * WC, WC), WC)
-
-            def block(i, _):
-                r = rows_of(1 - x, i)
-                dup2[r, cols] = (dot_nt(g2[r], wd[s]) * dup2[r, cols].astype(f32)).astype(bf16)
-                return 0
-
-            lax.fori_loop(0, n_rb, block, 0)
-
-        stream(wd_copy, n_hid, body)
+        def body(cols):
+            dup2[far, cols] = (dot_nt(g2[far], w_dn2[cols]) * dup2[far, cols].astype(f32)).astype(bf16)
+
+        over(hidden, WC, body)
 
 
     cos, sin = cs[0:8], cs[8:16]
@@ -461,7 +446,8 @@
 
         @pl.when(odd == 0)
         def _():
-            qkv_s[...] = dot_nt(w_t2[pair_q], h2[...]) + bq_s[pair_q, 0:1]
+            bias = jnp.broadcast_to(bq[pl.ds(pl.multiple_of(j * 2 * hq, 128), 2 * hq)][None], (128, 2 * hq)).T
+            qkv_s[...] = dot_nt(w_t2[pair_q], h2[...]) + bias[:, 0:1]
             do_s[...] = dot_nt(wo2[pair_v], g2[...]).astype(bf16)
 
         part = lambda i: qkv_s[pl.ds(pl.multiple_of(odd * hq + i * HD, HD), HD)]
@@ -489,12 +475,14 @@
 
 
     def xcopy(which, i):
-        dst = h2
-        r = pl.ds(pl.multiple_of(which * half + i * rb, rb), rb)
+        there = act2.at[rows_of(x, i), pl.ds(which * width, width)]
         return pltpu.make_async_remote_copy(
-            src_ref=fw.at[which, i], dst_ref=dst.at[r], send_sem=x_ss.at[which, i], recv_sem=x_rs.at[which, i],
+            src_ref=ag.at[which, i], dst_ref=there, send_sem=x_ss.at[which, i], recv_sem=x_rs.at[which, i],
             device_id=xp, device_id_type=MESH,
         )
+
+    def arrived(which, i):
+        return act2.at[rows_of(1 - x, i), pl.ds(which * width, width)]
 
     def each(body):
         def step(i, _):
@@ -503,88 +491,64 @@
 
         lax.fori_loop(0, n_rb, step, 0)
 
-    def branch(who, total):
-        def start(i, here):
-            total[here] = dot(att_t[:, rows_of(who, i)].T, wo2[...])
-
-        each(start)
-
-        def body(n, s):
-            cols = pl.ds(pl.multiple_of(n * WC, WC), WC)
-
-            def block(i, here):
-                total[here] = total[here] + dot(act2[rows_of(who, i), cols], wd[s])
-
-            each(block)
-
-        stream(wd_copy, n_hid, body)
-
-    def back(who, total):
-        def start(i, here):
-            total[here] = dot(dqkv_t[:, rows_of(who, i)].T, w_t2[...])
-
-        each(start)
-
-        def body(n, s):
-            cols = pl.ds(pl.multiple_of(n * WC, WC), WC)
-
-            def block(i, here):
-                total[here] = total[here] + dot_nt(dup2[rows_of(who, i), cols], wu[s])
-
-            each(block)
-
-        stream(wu_copy, n_hid, body)
-
-        def add_sums(i, here):
-            _, normed, _ = norm(rows_of(who, i))
-            d = total[here]
+    def branch_ff_far():
+        def body(cols):
+            acc[:, cols] = dot(act2[far], w_dn2[:, cols])
+
+        over(width, WC, body)
+
+    def back(who):
+        def rows(i, here):
+            r = rows_of(who, i)
+            tq[...] = dqkv_t[:, r].T
+            _, normed, _ = norm(r)
+
+            def body(cols):
+                acc[here, cols] = dot(tq[...], w_t2[:, cols]) + dot_nt(dup2[r], w_up2[cols])
+
+            over(width, WC, body)
+            d = acc[here]
             sums[0:1] = sums[0:1] + jnp.sum(d * normed, axis=0, keepdims=True)
             sums[1:2] = sums[1:2] + jnp.sum(d, axis=0, keepdims=True)
-
-        each(add_sums)
+            if who is not x:
+                ag[1, i] = d.astype(bf16)
+                xcopy(1, i).start()
+
+        each(rows)
 
     def out_copy():
-        return pltpu.make_async_copy(h2.at[pl.ds(0, half)], out, out_sem.at[0])
+        return pltpu.make_async_copy(act2.at[far, pl.ds(0, width)], out, out_sem.at[0])
 
     def branch_far():
-        branch(1 - x, acc)
         pl.semaphore_wait(free_sem, 1)
 
         def send(i, here):
-            fw[0, i] = acc[here].astype(bf16)
+            ag[0, i] = (acc[here] + dot(att_t[:, rows_of(1 - x, i)].T, wo2[...])).astype(bf16)
             xcopy(0, i).start()
-
-        each(send)
-
-    def back_far():
-        back(1 - x, acc)
-
-        def send(i, here):
-            fw[1, i] = acc[here].astype(bf16)
-            xcopy(1, i).start()
 
         each(send)
 
     def branch_near():
         for i in range(n_rb):
             r = rows_of(x, i)
-            acc2[...] = dot(att_t[:, r].T, wo2[...]) + (b_out[...] + b_down[...])
-
-            def body(n, s):
-                cols = pl.ds(pl.multiple_of(n * WC, WC), WC)
-                acc2[...] = acc2[...] + dot(act2[r, cols], wd[s])
-
-            stream(wd_copy, n_hid, body)
             xcopy(0, i).wait_recv()
-            here = pl.ds(i * rb, rb)
-            h2[here] = (r2[r].astype(f32) + acc2[...] + h2[here].astype(f32)).astype(bf16)
+            at = att_t[:, r].T
+            t_buf[:, 0 : at.shape[1]] = at
+
+            def body(cols):
+                total = dot(t_buf[:, 0 : at.shape[1]], wo2[:, cols]) + dot(act2[r, :], w_dn2[:, cols])
+                total = total + (b_out[cols] + b_down[cols])[None] + r2[r, cols].astype(f32)
+                there = act2.at[rows_of(1 - x, i), cols]
+                there[...] = (total + there[...].astype(f32)).astype(bf16)
+
+            over(width, WC, body)
         out_copy().start()
 
     def finish():
         def last(i, here):
             xcopy(1, i).wait_recv()
             _, normed, inv = norm(rows_of(x, i))
-            d_hat = (acc[here] + h2[pl.ds(pl.multiple_of(half + i * rb, rb), rb)].astype(f32)) * ln_gain[...]
+            d_hat = (acc[here] + arrived(1, i)[...].astype(f32)) * ln_gain[...][None]
             first = jnp.mean(d_hat, axis=1, keepdims=True)
             second = jnp.mean(d_hat * normed, axis=1, keepdims=True)
             acc[here] = g2[rows_of(x, i)].astype(f32) + inv * (d_hat - first - normed * second)
@@ -592,24 +556,14 @@
         each(last)
         pltpu.make_async_copy(acc, grad_in, out_sem.at[1]).start()
 
-    def column_sums(ref, k):
-        parts = []
-        for p in range(2):
-            parts.append(
-                lax.fori_loop(
-                    0, half // 128,
-                    lambda i, t: t + jnp.sum(ref[pl.ds(pl.multiple_of(p * half + i * 128, 128), 128), k].astype(f32), axis=0, keepdims=True),
-                    jnp.zeros((1, width), f32),
-                )
-            )
-        return parts[0] + parts[1]
-
     def small_fill():
         n_up = hidden // width
+        ones = jnp.ones((8, 2 * half), bf16)
+        up = dot(ones, dup2[...])
         for i in range(n_up):
-            sm_send[0, i : i + 1] = column_sums(dup2, slice(i * width, (i + 1) * width))
-        sm_send[0, n_up : n_up + 1] = column_sums(g2, slice(0, width))
-        bias = dot_nt(jnp.ones((8, 2 * half), bf16), dqkv_t[...])
+            sm_send[0, i : i + 1] = up[0:1, i * width : (i + 1) * width]
+        sm_send[0, n_up : n_up + 1] = dot(ones, g2[...])[0:1]
+        bias = dot_nt(ones, dqkv_t[...])
         sm_send[0, 3:4] = bias[0:1, :width]
         sm_send[0, 4:5, 0 : bias.shape[1] - width] = bias[0:1, width:]
 
@@ -623,11 +577,13 @@
 
     sums[...] = jnp.zeros_like(sums)
     sm_send[0] = jnp.zeros_like(sums)
+    loads[0].wait()
     turn_weights()
-    loads[0].wait()
     loads[1].wait()
     for i in range(n_rb):
         make_hidden(rows_of(x, i))
+    for i in range(2, 5):
+        loads[i].wait()
     ff_near()
     for i in range(n_rb):
         ff_far(i)
@@ -635,53 +591,69 @@
             r_copy(n_rb - 1, 1 - x).wait_send()
             for k in range(n_g):
                 g_copy(k).start()
-    loads[2].wait()
+    loads[5].wait()
     ff_wave(0)
 
-    def tick(t, _):
-        for s in range(6, 0, -1):
-            stage(s, t)
-
-        @pl.when(t == n_g - 1)
+    def turn_of(v, _):
+        t = v // len(TURNS)
+        for r, stages in enumerate(TURNS):
+
+            @pl.when(lax.rem(v, len(TURNS)) == r)
+            def _():
+                for k in stages:
+                    stage(k, t)
+
+        at = lambda k: pl.when(v == PLAN[k])
+
+        @at("branch_ff")
+        def _():
+            branch_ff_far()
+
+        @at("free")
+        def _():
+            pl.semaphore_signal(free_sem, inc=1, device_id=xp, device_id_type=MESH)
+
+        @at("d_up")
         def _():
             d_up_far()
 
-        @pl.when(t + 1 < n_ff)
-        def _():
-            ff_wave(t + 1)
-
-        done = sum(jnp.where(t > k, 1, 0) for k in HEAD_TICKS)
-        todo = sum(jnp.where(t >= k, 1, 0) for k in HEAD_TICKS)
-
-        def one(i, _):
-            head(i)
-            return 0
-
-        lax.fori_loop(done, todo, one, 0)
-        at = lambda k: pl.when(t == LATE + k)
-
-        @at(0)
-        def _():
-            pl.semaphore_signal(free_sem, inc=1, device_id=xp, device_id_type=MESH)
-            p_ff(n_ff - 2).wait_send()
-            p_ff(n_ff - 1).wait_send()
+        done = sum(jnp.where(v > k, 1, 0) for k in FF_AT)
+        todo = sum(jnp.where(v >= k, 1, 0) for k in FF_AT)
+
+        @pl.when(todo > done)
+        def _():
+            ff_wave(todo)
+
+        done_h = sum(jnp.where(v > k, 1, 0) for k in HEAD_AT)
+        todo_h = sum(jnp.where(v >= k, 1, 0) for k in HEAD_AT)
+
+        @pl.when(todo_h > done_h)
+        def _():
+            head(done_h)
+
+        @at("branch_far")
+        def _():
+            for i in range(NP):
+                p_at(n_at - NP + i).wait_send()
             branch_far()
-            back_far()
-
-        @at(1)
-        def _():
-            back(x, acc)
+
+        @at("back_far")
+        def _():
+            back(1 - x)
+
+        @at("back_near")
+        def _():
+            back(x)
+
+        @at("small")
+        def _():
             small_fill()
             sm_send[0, 5:7] = sums[0:2]
             small(0).start()
 
-        @at(2)
-        def _():
-            branch_near()
-
         for k in range(1, 6):
 
-            @at(1 + k)
+            @pl.when(v == SMALL_AT[k - 1])
             def _():
                 small(k - 1).wait_recv()
                 total = sm_send[k - 1] + sm_recv[k - 1]
@@ -695,35 +667,33 @@
                 else:
                     small_out[5:7] = total[5:7]
 
-        @at(5)
+        @at("branch_near")
+        def _():
+            branch_near()
+
+        @at("finish")
         def _():
             finish()
 
         return 0
 
-    lax.fori_loop(0, waves + 5, tick, 0)
+    lax.fori_loop(0, len(TURNS) * (waves + 5), turn_of, 0)
 
     def drain(w, _):
-        cp("A1", w).wait_send()
         cp("A5", w).wait_send()
         cp("G", w).wait()
         local(w).wait()
 
-        @pl.when(outer)
-        def _():
-            cp("B1", w).wait_send()
-            cp("A2", w).wait_send()
-
         @pl.when(inner)
         def _():
-            for k in ("B2", "A3", "B3", "A4", "B4", "B5a", "B5b"):
+            for k in ("A4", "B4", "B5a", "B5b"):
                 cp(k, w).wait_send()
 
         return 0
 
     lax.fori_loop(0, waves, drain, 0)
-    for i in range(NP):
-        p_at(n_at - NP + i).wait_send()
+    p_ff(n_ff - 2).wait_send()
+    p_ff(n_ff - 1).wait_send()
     for i in range(n_rb):
         xcopy(0, i).wait_send()
         xcopy(1, i).wait_send()
@@ -762,88 +732,138 @@
         ],
         scratch_shapes=[
             v16(rows, hidden), v16(rows, hidden), v16(rows, width), v16(rows, width), v16(rows, width),
-            v16(heads * 3 * HD, width), v16(heads * HD, width),
-            v16(waves, RW, width), v16(2, 2, RW, width), v16(NP, 2, RW, width), v16(waves, RW, width),
+            v16(heads * 3 * HD, width), v16(heads * HD, width), v16(width, hidden), v16(hidden, width),
+            v16(waves, RW, width), v16(2, 2, RW, width), v16(NP, 2, RW, width),
             v16(NS, RQ, width), v16(NS, RQ, width), v16(NS, RQ, width), v16(NS, 2 * RQ, width), v16(NS, RQ, width), v16(NS, RQ, width),
             v32(6 * HD, rows), v16(2 * HD, rows), v16(heads * 3 * HD, rows), v16(heads * HD, rows), v16(RW, rows),
-            v32(heads * 3 * HD, 128), v32(half, width), v32(256, width),
-            v16(2, WC, width), v16(2, width, WC),
+            v16(256, heads * 3 * HD), v32(half, width),
             v32(5, 8, width), v32(5, 8, width), v32(8, width),
             dma((len(KINDS), waves)), dma((len(KINDS), waves)), dma((waves,)), dma((N_LOADS,)), dma((n_rb,)), dma((n_rb,)),
-            dma((n_g,)), dma((n_g,)), dma((2, n_rb)), dma((2, n_rb)), dma((2,)), dma((2,)), dma((5,)), dma((5,)), dma((2,)), pltpu.SemaphoreType.REGULAR,
-        ],
+            dma((n_g,)), dma((n_g,)), dma((2, n_rb)), dma((2, n_rb)), dma((5,)), dma((5,)), dma((2,))] + [pltpu.SemaphoreType.REGULAR] * 4,
         compiler_params=pltpu.CompilerParams(collective_id=0, has_side_effects=True, vmem_limit_bytes=63 * 2**20),
         name="attention_and_sums",
     )(g_n, r_n, w_qkv, wo, w_up, w_down, *small)
 
 
-def widen_kernel(n_g, src, down, up, qkv, out):
-    i = pl.program_id(0)
-    width = src.shape[2]
-    side = lambda k: lax.broadcasted_iota(jnp.int32, (RW, RW), k)
-    eye = jnp.where(side(0) == side(1), 1.0, 0.0).astype(bf16)
-
-    @pl.when(i < n_g)
-    def _():
+def widen_kernel(
+    n_g, n_at, src, out_in, grad_in, small, down, up, qkv, proj, out, grad, g_gain, g_bias, g_qkv, g_out, g_down, g_up,
+    buf, wide, wide_q, wide_p, buf_o, buf_g, in_sem, sem, q_sem, p_sem, through_sem,
+):
+    waves, _, width = src.shape
+    hq = 3 * HD
+    arrive = [pltpu.make_async_copy(a, b, through_sem.at[i]) for i, (a, b) in enumerate(((out_in, buf_o), (grad_in, buf_g)))]
+    leave = [pltpu.make_async_copy(a, b, through_sem.at[2 + i]) for i, (a, b) in enumerate(((buf_o, out), (buf_g, grad)))]
+    loads = [pltpu.make_async_copy(src.at[w], buf.at[w], in_sem.at[w]) for w in range(waves)]
+    for k in arrive + loads:
+        k.start()
+    row = lax.broadcasted_iota(jnp.int32, (RW, RW), 0)
+    eye = jnp.where(row == lax.broadcasted_iota(jnp.int32, (RW, RW), 1), 1.0, 0.0).astype(bf16)
+    slots, busy, used = wide.shape[0], {}, 0
+    for a, b in zip(arrive, leave):
+        a.wait()
+        b.start()
+
+    def free(slot):
+        for k in busy.pop(slot, []):
+            k.wait()
+
+    def send(slot, copies):
+        for k in copies:
+            k.start()
+        busy[slot] = copies
+
+    for w in range(waves):
+        loads[w].wait()
+        if n_g <= w < n_g + n_at:
+            j = w - n_g
+            s = j % 2
+            free(("q", s))
+            for k in range(width // RW):
+                cols = slice(k * RW, (k + 1) * RW)
+                both = jnp.concatenate([buf[w, 0:hq, cols], buf[w, RW : RW + hq, cols]], axis=0)
+                wide_q[s, cols] = dot_nt(eye, both)
+            for c in range(2):
+                wide_p[s, c * HD : (c + 1) * HD] = buf[w, c * RW + hq : (c + 1) * RW].astype(f32)
+            send(("q", s), [
+                pltpu.make_async_copy(wide_q.at[s], qkv.at[:, pl.ds(j * 2 * hq, 2 * hq)], q_sem.at[s]),
+                pltpu.make_async_copy(wide_p.at[s], proj.at[pl.ds(j * 2 * HD, 2 * HD)], p_sem.at[s]),
+            ])
+            continue
+        s = used % slots
+        used += 1
+        free(s)
+        copies = []
         for c in range(2):
-            for k in range(width // RW):
-                down[c * width + k * RW : c * width + (k + 1) * RW] = dot_nt(
-                    eye, src[0, c * RW : (c + 1) * RW, k * RW : (k + 1) * RW]
-                )
-
-    @pl.when(jnp.logical_and(i >= n_g, i < 2 * n_g))
-    def _():
-        for c in range(2):
-            up[:, c * width : (c + 1) * width] = src[0, c * RW : (c + 1) * RW].astype(f32)
-
-    @pl.when(i >= 2 * n_g)
-    def _():
-        hq = 3 * HD
-        for k in range(width // RW):
-            cols = slice(k * RW, (k + 1) * RW)
-            both = jnp.concatenate([src[0, 0:hq, cols], src[0, RW : RW + hq, cols]], axis=0)
-            qkv[cols] = dot_nt(eye, both)
-        for c in range(2):
-            out[c * HD : (c + 1) * HD] = src[0, c * RW + hq : (c + 1) * RW].astype(f32)
-
-
-def widen(red, hidden):
+            if w < n_g:
+                for k in range(width // RW):
+                    n = c * (width // RW) + k
+                    cols = slice(n * RW, (n + 1) * RW)
+                    wide[s, :, cols] = dot_nt(eye, buf[w, c * RW : (c + 1) * RW, k * RW : (k + 1) * RW])
+                    copies.append(
+                        pltpu.make_async_copy(
+                            wide.at[s, :, cols], down.at[cols, pl.ds(w * RW, RW)], sem.at[s, n]
+                        )
+                    )
+            else:
+                wide[s, :, c * width : (c + 1) * width] = buf[w, c * RW : (c + 1) * RW].astype(f32)
+        if w >= n_g:
+            copies = [pltpu.make_async_copy(wide.at[s], up.at[pl.ds((w - n_g - n_at) * RW, RW)], sem.at[s, 0])]
+        send(s, copies)
+    n_up = g_up.shape[0] // width
+    for i in range(n_up):
+        g_up[i * width : (i + 1) * width] = small[i]
+    g_out[...] = small[n_up]
+    g_down[...] = small[n_up]
+    g_qkv[0:width] = small[3]
+    g_qkv[width:] = small[4, 0 : g_qkv.shape[0] - width]
+    g_gain[...] = small[5]
+    g_bias[...] = small[6]
+    for s in list(busy):
+        free(s)
+    for k in leave:
+        k.wait()
+
+
+def widen(red, out, grad_in, small, hidden):
     waves, _, width = red.shape
     n_g = width // RW
     n_at = waves - 2 * n_g
-    clip = lambda i, first, n: jnp.minimum(jnp.maximum(i - first, 0), n - 1)
+    vm = pl.BlockSpec(memory_space=pltpu.VMEM)
+    hbm = pl.BlockSpec(memory_space=pl.ANY)
+    dma = pltpu.SemaphoreType.DMA
+    s32 = lambda *s: jax.ShapeDtypeStruct(s, f32)
     return pl.pallas_call(
-        functools.partial(widen_kernel, n_g),
-        grid=(waves,),
-        in_specs=[pl.BlockSpec((1, 2 * RW, width), lambda i: (i, 0, 0))],
-        out_specs=[
-            pl.BlockSpec((hidden, RW), lambda i: (0, clip(i, 0, n_g))),
-            pl.BlockSpec((RW, hidden), lambda i: (clip(i, n_g, n_g), 0)),
-            pl.BlockSpec((width, 6 * HD), lambda i: (0, clip(i, 2 * n_g, n_at))),
-            pl.BlockSpec((2 * HD, width), lambda i: (clip(i, 2 * n_g, n_at), 0)),
+        functools.partial(widen_kernel, n_g, n_at),
+        in_specs=[hbm] * 3 + [vm],
+        out_specs=[hbm] * 6 + [vm] * 6,
+        out_shape=[
+            s32(hidden, width), s32(width, hidden), s32(width, n_at * 6 * HD), s32(n_at * 2 * HD, width),
+            jax.ShapeDtypeStruct(out.shape, out.dtype), s32(*grad_in.shape),
+            s32(width), s32(width), s32(n_at * 6 * HD), s32(width), s32(width), s32(hidden),
         ],
-        out_shape=[
-            jax.ShapeDtypeStruct((hidden, width), f32),
-            jax.ShapeDtypeStruct((width, hidden), f32),
-            jax.ShapeDtypeStruct((width, n_at * 6 * HD), f32),
-            jax.ShapeDtypeStruct((n_at * 2 * HD, width), f32),
+        scratch_shapes=[
+            pltpu.VMEM((waves, 2 * RW, width), bf16), pltpu.VMEM((4, RW, hidden), f32), pltpu.VMEM((2, width, 6 * HD), f32),
+            pltpu.VMEM((2, 2 * HD, width), f32), pltpu.VMEM(out.shape, out.dtype), pltpu.VMEM(grad_in.shape, f32),
+            dma((waves,)), dma((4, hidden // RW)), dma((2,)), dma((2,)), dma((4,)),
         ],
-        compiler_params=pltpu.CompilerParams(vmem_limit_bytes=48 * 2**20),
+        compiler_params=pltpu.CompilerParams(vmem_limit_bytes=56 * 2**20),
         name="widen",
-    )(red)
+    )(red, out, grad_in, small)
 
 
 def shards(residual, ln_gain, ln_bias, w_qkv, b_qkv, w_out, b_out, w_up, b_up, w_down, b_down, grad_out):
-    width = residual.shape[1]
-    cosine, sine = turn_tables(2 * residual.shape[0])
-    cs = jnp.concatenate([cosine.T, sine.T])
-    rows = [v[None] for v in (b_qkv, b_up)] + [cs] + [v[None] for v in (ln_gain, ln_bias, b_out, b_down)]
-    red, out, grad_in, small = mega(grad_out, residual, w_qkv, w_out, w_up, w_down, *rows)
-    grad_w_down, grad_w_up, grad_w_qkv, grad_w_out = widen(red, w_down.shape[0])
-    gb_up = small[: b_up.shape[0] // width].reshape(-1)
-    gb_out = small[2]
-    gb_qkv = small[3:5].reshape(-1)[: b_qkv.shape[0]]
-    return out, grad_in, small[5], small[6], grad_w_qkv, gb_qkv, grad_w_out, gb_out, grad_w_up, gb_up, grad_w_down, gb_out
+    rows = 2 * residual.shape[0]
+    half_rot = ROT // 2
+    inverse = 1.0 / np.float32(10000.0) ** (np.arange(half_rot, dtype=np.float32) * np.float32(2.0 / ROT))
+    angles = np.arange(rows, dtype=np.float32)[None, :] * inverse[:, None].astype(np.float32)
+    cs = jnp.asarray(np.concatenate([np.cos(angles), np.sin(angles)]).astype(np.float32))
+    red, out, grad_in, small = mega(
+        grad_out, residual, w_qkv, w_out, w_up, w_down, b_qkv, b_up, cs, ln_gain, ln_bias, b_out, b_down
+    )
+    grad_w_down, grad_w_up, grad_w_qkv, grad_w_out, out, grad_in, gain, bias, gb_qkv, gb_out, gb_down, gb_up = widen(
+        red, out, grad_in, small, w_down.shape[0]
+    )
+    return out, grad_in, gain, bias, grad_w_qkv, gb_qkv, grad_w_out, gb_out, grad_w_up, gb_up, grad_w_down, gb_down
 
 
 def contract_rows(left, right):

time: 228 us -> 202 us (0.89)
  Pallas kernels: 218 us -> 200 us
  local copies, waits for them, and re-layouts: 7.11 us -> 0 us
    pallas_call x1, Pallas kernels: 200 us -> 184 us  [mega(): pl.pallas_call(functools.partial(mega_kernel, heads), in_specs=[hbm] * 6...]
    unnamed x10 -> x0, local copies, waits for them, and re-layouts: 3.73 us -> none
where the time goes in v3:
time: 202 us; the launch traced here: 201 us
  Pallas kernels  200 us (99%)
    pallas_call x1, Pallas kernels, mega(): pl.pallas_call(functools.partial(mega_kernel, heads), in_specs=[hbm] * 6...  184 us
    pallas_call x1, Pallas kernels, widen(): pl.pallas_call(functools.partial(widen_kernel, n_g, n_at), in_specs=[hbm]...  16.6 us

profile of v3, /device:TPU:0, one launch (start us, length us, event | category | flops | bytes accessed | tf_op | source)
XLA Modules:
  0.0 201.3 jit_solution(14603937441819098576)
XLA Ops:
  0.6 183.9 %attention_and_sums.1 = (bf16[12,512,1024]{2,1,0:T(8,128)(2,1)}, bf16[512,1024]{1,0:T(8,128)(2,1)}, f32[512,1024]{1,0:T(8,128)}, f32[8,1024]{1,0:T(8,128)}) custom-call(bf16[512,1024]{1,0:T(8,128)(2,1)} %g_n.1, bf16[512,1024]{1,0:T(8,128)(2,1)} %r_n.1, bf16[1024,1536]{1,0:T(8,128)(2,1)} %w_qkv.1, bf16[512,1024]{1,0:T(8,128)(2,1)} %wo.1, ...), custom_call_target="tpu_custom_call" | custom-call | tf_op jit(solution)/shard_map/attention_and_sums/pallas_call | solution.py:723
  184.5 16.6 %widen.1 = (f32[2048,1024]{1,0:T(8,128)}, f32[1024,2048]{1,0:T(8,128)}, f32[1024,1536]{1,0:T(8,128)}, f32[512,1024]{1,0:T(8,128)}, bf16[512,1024]{1,0:T(8,128)(2...) custom-call(bf16[12,512,1024]{2,1,0:T(8,128)(2,1)} %get-tuple-elemen, ...), custom_call_target="tpu_custom_call" | custom-call | tf_op jit(solution)/shard_map/widen/pallas_call | solution.py:835

commit v4 on v3

--- a/solution.py
+++ b/solution.py
@@ -104,7 +104,7 @@
 FF_AT = (1, 4, 7, 22, 24, 27, 30)
 HEAD_AT = (8, 9, 10, 12, 13, 15, 16, 18)
 PLAN = {
-    "branch_ff": 0, "free": 12, "d_up": 19, "branch_far": 21, "back_far": 25, "back_near": 28, "small": 31,
+    "branch_ff": 5, "free": 12, "d_up": 19, "branch_far": 21, "back_far": 25, "back_near": 28, "small": 31,
     "branch_near": 36, "finish": 45,
 }
 SMALL_AT = (34, 37, 40, 43, 46)

time: 202 us -> 200 us (0.990)
  no operation moved by 1% of the time
where the time goes in v4:
time: 200 us
  Pallas kernels  199 us (100%)
    pallas_call x1, Pallas kernels, mega(): pl.pallas_call(functools.partial(mega_kernel, heads), in_specs=[hbm] * 6...  182 us
    pallas_call x1, Pallas kernels, widen(): pl.pallas_call(functools.partial(widen_kernel, n_g, n_at), in_specs=[hbm]...  16.6 us

profile of v4, /device:TPU:0, one launch (start us, length us, event | category | flops | bytes accessed | tf_op | source)
XLA Modules:
  0.0 199.7 jit_solution(2622363373829348386)
XLA Ops:
  0.6 182.3 %attention_and_sums.1 = (bf16[12,512,1024]{2,1,0:T(8,128)(2,1)}, bf16[512,1024]{1,0:T(8,128)(2,1)}, f32[512,1024]{1,0:T(8,128)}, f32[8,1024]{1,0:T(8,128)}) custom-call(bf16[512,1024]{1,0:T(8,128)(2,1)} %g_n.1, bf16[512,1024]{1,0:T(8,128)(2,1)} %r_n.1, bf16[1024,1536]{1,0:T(8,128)(2,1)} %w_qkv.1, bf16[512,1024]{1,0:T(8,128)(2,1)} %wo.1, ...), custom_call_target="tpu_custom_call" | custom-call | tf_op jit(solution)/shard_map/attention_and_sums/pallas_call | solution.py:723
  182.9 16.6 %widen.1 = (f32[2048,1024]{1,0:T(8,128)}, f32[1024,2048]{1,0:T(8,128)}, f32[1024,1536]{1,0:T(8,128)}, f32[512,1024]{1,0:T(8,128)}, bf16[512,1024]{1,0:T(8,128)(2...) custom-call(bf16[12,512,1024]{2,1,0:T(8,128)(2,1)} %get-tuple-elemen, ...), custom_call_target="tpu_custom_call" | custom-call | tf_op jit(solution)/shard_map/widen/pallas_call | solution.py:835
